TPU v7x, 32 devices: a whole 2x2x4 slice. The times are simulated.
32 devices in a mesh: fsdp: 8 (over z, y), tp: 4 (over x, core).
Axes of the slice: x: 2, y: 2, z: 4, core: 2. Of those that a mesh axis runs over, the one named last changes fastest.
Arguments:
- tokens: bfloat16 [8192, 1024], P(('fsdp', 'tp')), may hold values from -6 to 6
- segment_ids: int32 [8192], P('fsdp'), may hold values from 0 to 127, as said below
- cotangent: bfloat16 [8192, 1024], P(('fsdp', 'tp')), may hold values from -6 to 6
- norm_gain: float32 [1024], P(('fsdp', 'tp')), may hold values from 0.5 to 1.5
- w_z: float32 [1024, 1536], P('fsdp', 'tp'), may hold values from -0.09375 to 0.09375, as said below
- w_x: float32 [1024, 1536], P('fsdp', 'tp'), may hold values from -0.09375 to 0.09375, as said below
- w_bc: float32 [1024, 256], P(('fsdp', 'tp')), may hold values from -0.09375 to 0.09375, as said below
- w_dt: float32 [1024, 24], P('fsdp', 'tp'), may hold values from -0.09375 to 0.09375, as said below
- conv_x: float32 [1536, 4], P('tp'), may hold values from -3 to 3
- conv_bias_x: float32 [1536], P('tp'), may hold values from -1.75 to 1.75
- conv_bc: float32 [256, 4], P(('fsdp', 'tp')), may hold values from -3 to 3
- conv_bias_bc: float32 [256], P(('fsdp', 'tp')), may hold values from -1.75 to 1.75
- dt_bias: float32 [24], P('tp'), may hold values from -6 to -2
- a_log: float32 [24], P('tp'), may hold values from 0 to 2.75
- d_skip: float32 [24], P('tp'), may hold values from 0.5 to 1.5
- mixer_gain: float32 [1536], P('tp'), may hold values from 0.5 to 1.5
- w_mixer_out: float32 [1536, 1024], P('tp', 'fsdp'), may hold values from -0.15625 to 0.15625
- w_query: float32 [1024, 512], P('fsdp', 'tp'), may hold values from -0.09375 to 0.09375, as said below
- w_keyval: float32 [1024, 256], P(('fsdp', 'tp')), may hold values from -0.09375 to 0.09375, as said below
- w_attn_out: float32 [512, 1024], P('tp', 'fsdp'), may hold values from -0.75 to 0.75
- ffn_gain: float32 [1024], P(('fsdp', 'tp')), may hold values from 0.5 to 1.5
- w_gate: float32 [1024, 2048], P('fsdp', 'tp'), may hold values from -0.1875 to 0.1875
- w_up: float32 [1024, 2048], P('fsdp', 'tp'), may hold values from -0.1875 to 0.1875
- w_down: float32 [2048, 1024], P('tp', 'fsdp'), may hold values from -0.125 to 0.125
Outputs:
- layer_out: bfloat16 [8192, 1024], P(('fsdp', 'tp'))
- grad_tokens: float32 [8192, 1024], P(('fsdp', 'tp'))
- grad_norm_gain: float32 [1024], P(('fsdp', 'tp'))
- grad_w_z: float32 [1024, 1536], P('fsdp', 'tp')
- grad_w_x: float32 [1024, 1536], P('fsdp', 'tp')
- grad_w_bc: float32 [1024, 256], P(('fsdp', 'tp'))
- grad_w_dt: float32 [1024, 24], P('fsdp', 'tp')
- grad_conv_x: float32 [1536, 4], P('tp')
- grad_conv_bias_x: float32 [1536], P('tp')
- grad_conv_bc: float32 [256, 4], P(('fsdp', 'tp'))
- grad_conv_bias_bc: float32 [256], P(('fsdp', 'tp'))
- grad_dt_bias: float32 [24], P('tp')
- grad_a_log: float32 [24], P('tp')
- grad_d_skip: float32 [24], P('tp')
- grad_mixer_gain: float32 [1536], P('tp')
- grad_w_mixer_out: float32 [1536, 1024], P('tp', 'fsdp')
- grad_w_query: float32 [1024, 512], P('fsdp', 'tp')
- grad_w_keyval: float32 [1024, 256], P(('fsdp', 'tp'))
- grad_w_attn_out: float32 [512, 1024], P('tp', 'fsdp')
- grad_ffn_gain: float32 [1024], P(('fsdp', 'tp'))
- grad_w_gate: float32 [1024, 2048], P('fsdp', 'tp')
- grad_w_up: float32 [1024, 2048], P('fsdp', 'tp')
- grad_w_down: float32 [2048, 1024], P('tp', 'fsdp')
Inputs may be any that keep to these rules, and one draw needn't show every extreme that they name: `segment_ids`: within each sequence of 1024 tokens the ids start at 0 and rise by 0 or 1 from one token to the next; they rise only at positions that are multiples of 8 within the sequence. `w_z`: independent entries of deviation 1024^-0.5. `w_x`: independent entries of deviation 1024^-0.5. `w_bc`: independent entries of deviation 1024^-0.5. `w_dt`: independent entries of deviation 1024^-0.5. `w_query`: independent entries of deviation 1024^-0.5. `w_keyval`: independent entries of deviation 1024^-0.5.
All inputs are finite; a program needn't handle non-finite values.
Results may differ from a plain program's by a relative error of at most 0.025.
Values may be sent and summed in bfloat16 or wider, within the bound.
No kernel may reach another device: no remote copies, remote signals or barrier semaphores. Data moves between devices by JAX's collectives and lax.ppermute only.
A program may use at most 192 MiB of HBM per device.

v0:
```python
import functools

import jax
import jax.numpy as jnp
from jax import lax
from jax.experimental import pallas as pl
from jax.experimental.pallas import tpu as pltpu
from jax.sharding import PartitionSpec as P

STATE = 128
CONV = 4
HEADS = 8
KV_HEADS = 2
HEAD = 64

EPS = 1e-06
ROPE_BASE = 10000.0
NEG_FILL = -1e30
LOG2_E = 1.4426950408889634


def contract_rows(left_side, right_side):
    return lax.dot_general(
        left_side, right_side, (((0,), (0,)), ((), ())), preferred_element_type=jnp.float32
    )


def contract_cols(left_side, right_side):
    return lax.dot_general(
        left_side, right_side, (((1,), (1,)), ((), ())), preferred_element_type=jnp.float32
    )


def split_cols(matrix, widths):
    pieces = []
    begin_at = 0
    for part_width in widths:
        pieces.append(matrix[:, begin_at : begin_at + part_width])
        begin_at = begin_at + part_width
    return pieces


def flip(values, axis, mask):
    size = lax.axis_size(axis)
    return lax.ppermute(values, axis, [(i, i ^ mask) for i in range(size)])


def ring(values, step):
    return lax.ppermute(values, "fsdp", [(i, (i + 2 * step) % 8) for i in range(8)])


def staged():
    return lax.axis_size("fsdp") == 8


def place_bits():
    index = lax.axis_index("tp")
    return index // 2, index % 2


def gather_pieces(rows_in, *deps):
    far = flip(rows_in, "tp", 2)
    near = flip(rows_in, "tp", 1)
    cross = flip(after(far, *deps), "tp", 1)
    return rows_in, far, near, cross


def reduce_pieces(keep, give, *deps):
    half = keep.shape[0] // 2
    near = flip(give, "tp", 1)
    passed = after((keep[half:] + near[half:].astype(jnp.float32)).astype(jnp.bfloat16), *deps)
    far = flip(passed, "tp", 2)
    return keep, near, far, passed


def fsdp_place():
    index = lax.axis_index("fsdp")
    return index // 2, index % 2


def after(value, *deps):
    if not deps:
        return value

    def body(_, value_ref, out_ref):
        out_ref[...] = value_ref[...]

    return call_kernel(
        body, [(value.shape, value.dtype)], [], no_scalar(), value, deps=deps, micros=1, limit=8
    )[0]


def no_scalar():
    return jnp.zeros((1,), jnp.int32)


def fetch_blocks(grads, rows, places, held, sems):
    copies = []
    for k, (grad, here) in enumerate(zip(grads, held)):
        for n, (dy, dz) in enumerate(places):
            copies.append(
                pltpu.make_async_copy(
                    grad.at[pl.ds((dy * 4 + dz) * rows, rows)],
                    here.at[pl.ds(n * rows, rows)],
                    sems.at[k * len(places) + n],
                )
            )
    for copy in copies:
        copy.start()

    def blocks(n):
        for k in range(len(grads)):
            copies[k * len(places) + n].wait()
        return [here[n * rows : n * rows + rows] for here in held]

    return blocks


def store_side_by_side(values, out_ref):
    begin_at = 0
    for value in values:
        out_ref[:, begin_at : begin_at + value.shape[1]] = value.astype(out_ref.dtype)
        begin_at = begin_at + value.shape[1]


def add_arrivals(values, arrivals):
    sums, begin_at = [], 0
    for value in values:
        columns = slice(begin_at, begin_at + value.shape[1])
        total = value.astype(jnp.float32)
        for arrival in arrivals:
            total = total + arrival[:, columns].astype(jnp.float32)
        sums.append(total)
        begin_at = begin_at + value.shape[1]
    return sums


def put_extra(values, out_ref, rows):
    width = out_ref.shape[1]
    halves = jnp.concatenate([values[:, :width], values[:, width:]], axis=0)
    out_ref[rows : rows + 16] = halves.astype(out_ref.dtype)


def get_extra(ref, rows):
    values = ref[rows : rows + 16].astype(jnp.float32)
    return jnp.concatenate([values[:8], values[8:]], axis=1)


def first_block_body(count, rows, extra, _, *refs):
    extra_ref, refs = (refs[0], refs[1:]) if extra else (None, refs)
    grads, out_ref, held, sems = refs[:count], refs[count], refs[count + 1 : -1], refs[-1]
    blocks = fetch_blocks(grads, rows, [(1, 3)], held, sems)
    if extra:
        put_extra(extra_ref[...], out_ref, rows)
    store_side_by_side(blocks(0), out_ref.at[:rows])


def step_body(count, arriving, rows, dz, extra, _, *refs):
    extra_ref, refs = (refs[0], refs[1:]) if extra else (None, refs)
    arrivals, refs = refs[:arriving], refs[arriving:]
    grads, (send_ref, next_ref), refs = refs[:count], refs[count : count + 2], refs[count + 2 :]
    if extra:
        extra_out, refs = refs[0], refs[1:]
    blocks = fetch_blocks(grads, rows, [(1, dz - 1), (0, dz)], refs[:-1], refs[-1])
    if extra:
        came = get_extra(arrivals[-1], rows)
        total = extra_ref[...] + came
        extra_out[...] = total
        put_extra(total if arriving == 1 else came, send_ref, rows)
        next_ref[rows : rows + 16] = jnp.zeros((16, next_ref.shape[1]), next_ref.dtype)
    store_side_by_side(blocks(0), next_ref.at[:rows])
    sums = add_arrivals(blocks(1), [ref[:rows] for ref in arrivals])
    store_side_by_side(sums, send_ref.at[:rows])


def total_body(count, rows, columns, weighted, arriving, extra, _, *refs):
    size = len(weighted)
    extra_ref, refs = (refs[0], refs[1:]) if extra else (None, refs)
    arrivals, refs = refs[:arriving], refs[arriving:]
    grads, weights, refs = refs[:count], refs[count : count + size], refs[count + size :]
    outs, by_row_ref = refs[: len(columns)], refs[len(columns)]
    if extra:
        refs[len(columns) + 1][...] = extra_ref[...] + get_extra(arrivals[-1], rows)
    held, sems = refs[len(columns) + 1 + extra : -1], refs[-1]
    arrivals = [ref[:rows] for ref in arrivals]
    blocks = fetch_blocks(grads, rows, [(0, 0)], held[:count], sems)
    held = held[count:]
    copies = [
        pltpu.make_async_copy(weight, here, sems.at[count + k])
        for k, (weight, here) in enumerate(zip(weights, held))
    ]
    for copy in copies:
        copy.start()
    sums = add_arrivals(blocks(0), arrivals)
    total = jnp.concatenate(sums, axis=1) if len(sums) > 1 else sums[0]
    for (begin_at, width, turned), out_ref in zip(columns, outs):
        values = total[:, begin_at : begin_at + width]
        out_ref[...] = values.T if turned else values
    by_row = jnp.zeros((total.shape[0], 1), jnp.float32)
    for (begin_at, offset, width), copy, here in zip(weighted, copies, held):
        copy.wait()
        values = total[:, begin_at : begin_at + width]
        rounded = here[:, offset : offset + width].astype(jnp.bfloat16).astype(jnp.float32)
        by_row = by_row + jnp.sum(values * rounded, axis=1, keepdims=True)
    by_row_ref[...] = jnp.broadcast_to(by_row, by_row_ref.shape)


class Scatter:
    def __init__(self, grads, *deps, extra=None):
        self.grads = grads
        self.rows = grads[0].shape[0] // 8
        self.width = sum(grad.shape[1] for grad in grads)
        self.arrivals = []
        self.ready = grads[0]
        self.extra = [] if extra is None else [extra]
        if staged():
            (first,) = call_kernel(
                functools.partial(first_block_body, len(grads), self.rows, len(self.extra)),
                [((self.rows + 16 * len(self.extra), self.width), jnp.bfloat16)],
                [((self.rows, grad.shape[1]), grad.dtype) for grad in grads],
                no_scalar(),
                *self.extra,
                *grads,
                deps=deps,
                micros=1,
                distant=len(grads),
                sems=len(grads),
            )
            self.ready = first
            self.arrivals = [flip(first, "fsdp", 1)]

    def step(self, dz, *deps):
        if not staged():
            return ()
        block = ((self.rows + 16 * len(self.extra), self.width), jnp.bfloat16)
        send, following, *self.extra = call_kernel(
            functools.partial(
                step_body, len(self.grads), len(self.arrivals), self.rows, dz, len(self.extra)
            ),
            [block, block] + [(extra.shape, extra.dtype) for extra in self.extra],
            [((2 * self.rows, grad.shape[1]), grad.dtype) for grad in self.grads],
            no_scalar(),
            *self.extra,
            *self.arrivals,
            *self.grads,
            deps=deps,
            micros=1,
            distant=len(self.grads),
            sems=2 * len(self.grads),
        )
        self.ready = send
        self.arrivals = [flip(following, "fsdp", 1), ring(send, 1)]
        return self.arrivals

    def total(self, columns, weighted, *weights, deps=()):
        extra = self.extra if staged() else []
        if staged():
            grads, rows = self.grads, self.rows
        else:
            grads = [
                lax.psum_scatter(
                    jnp.concatenate(self.grads, axis=1), "fsdp", scatter_dimension=0, tiled=True
                )
            ]
            rows = grads[0].shape[0]
        shapes = [
            ((width, rows) if turned else (rows, width), jnp.float32)
            for _, width, turned in columns
        ]
        outs = call_kernel(
            functools.partial(
                total_body, len(grads), rows, columns, weighted, len(self.arrivals), len(extra)
            ),
            shapes + [((rows, 128), jnp.float32)] + [(item.shape, item.dtype) for item in extra],
            [((rows, grad.shape[1]), grad.dtype) for grad in grads]
            + [(weight.shape, weight.dtype) for weight in weights],
            no_scalar(),
            *extra,
            *self.arrivals,
            *grads,
            *weights,
            deps=deps,
            micros=1,
            distant=len(grads) + len(weights),
            sems=len(grads) + len(weights),
        )
        if not staged():
            outs = list(outs) + [lax.psum(item, "fsdp") for item in self.extra]
        return outs


def join_columns(arrays, *deps):
    def body(_, *refs):
        store_side_by_side([ref[...] for ref in refs[:-1]], refs[-1])

    rows, width = arrays[0].shape[0], sum(array.shape[1] for array in arrays)
    outs = [((rows, width), arrays[0].dtype)]
    return call_kernel(body, outs, [], no_scalar(), *arrays, deps=deps, micros=1, limit=8)[0]


class Gather:
    def __init__(self, shard):
        self.shard = self.ready = shard
        if staged():
            self.along, self.across = [shard], []
        self.arrivals = []

    def step(self, *deps):
        if not staged():
            return ()
        held = self.ready = after(self.along[-1], *self.across[-1:], *deps)
        if len(self.along) < 4:
            self.along.append(ring(held, 1))
        self.across.append(flip(held, "fsdp", 1))
        self.arrivals = [self.along[-1], self.across[-1]]
        return self.arrivals

    def parts(self):
        if not staged():
            return [lax.all_gather(self.shard, "fsdp", axis=0, tiled=True)]
        return [blocks[-dz % 4] for blocks in (self.along, self.across) for dz in range(4)]


def sum_fsdp(values):
    if not staged():
        return lax.psum(values, "fsdp")
    for mask in (1, 2, 6):
        values = values + flip(values, "fsdp", mask)
    return values


def sum_tp(values):
    for mask in (1, 2):
        values = values + flip(values, "tp", mask)
    return values


def feature_order():
    if not staged():
        return jnp.arange(8, dtype=jnp.int32)
    z_at, y_at = fsdp_place()
    steps = jnp.arange(8, dtype=jnp.int32)
    return (z_at + steps % 4) % 4 * 2 + (y_at ^ (steps // 4))


CHUNK = 128


def row_chunks(rows, body, carry=0):
    def step(k, carry):
        return body(pl.ds(pl.multiple_of(k * CHUNK, CHUNK), CHUNK), carry)

    return lax.fori_loop(0, rows // CHUNK, step, carry)


def front_body(order_ref, tok_ref, cot_ref, normed_ref, tok_rel, cot_rel):
    rows_all, width = tok_ref.shape
    block = width // 8

    def chunk(rows, carry):
        for b in range(8):
            there = pl.ds(pl.multiple_of(order_ref[b] * block, block), block)
            here = slice(b * block, b * block + block)
            tok_rel[rows, here] = tok_ref[rows, there]
            cot_rel[rows, here] = cot_ref[rows, there]
        values = tok_rel[rows].astype(jnp.float32)
        normed = values * lax.rsqrt(jnp.mean(values * values, axis=-1, keepdims=True) + EPS)
        normed_ref[rows] = normed.astype(jnp.bfloat16)
        return carry

    row_chunks(rows_all, chunk)


def summed_rows(rows, keep_ref, near_ref, far_ref):
    return (
        keep_ref[rows] + near_ref[rows].astype(jnp.float32) + far_ref[rows].astype(jnp.float32)
    )


def mixed_body(_, tok_ref, keep_ref, near_ref, far_ref, gain_ref, after_ref, second_ref):
    def chunk(rows, carry):
        after = tok_ref[rows].astype(jnp.float32) + summed_rows(rows, keep_ref, near_ref, far_ref)
        after_ref[rows] = after
        normed = after * lax.rsqrt(jnp.mean(after * after, axis=-1, keepdims=True) + EPS)
        second_ref[rows] = (normed * gain_ref[...]).astype(jnp.bfloat16)
        return carry

    row_chunks(tok_ref.shape[0], chunk)


def output_body(order_ref, after_ref, keep_ref, near_ref, far_ref, out_ref):
    block = after_ref.shape[1] // 8

    def chunk(rows, carry):
        values = after_ref[rows] + summed_rows(rows, keep_ref, near_ref, far_ref)
        values = values.astype(jnp.bfloat16)
        for b in range(8):
            there = pl.ds(pl.multiple_of(order_ref[b] * block, block), block)
            out_ref[rows, there] = values[:, b * block : b * block + block]
        return carry

    row_chunks(after_ref.shape[0], chunk)


def norm_back(values, d_out, gain):
    inverse = lax.rsqrt(jnp.mean(values * values, axis=-1, keepdims=True) + EPS)
    normed = values * inverse
    scaled = d_out * gain
    return inverse * (scaled - normed * jnp.mean(scaled * normed, axis=-1, keepdims=True))


def after_back_body(
    _, after_ref, cot_ref, keep_ref, near_ref, far_ref, gain_ref, d_after_ref, d_mix_ref
):
    def chunk(rows, carry):
        d_second = summed_rows(rows, keep_ref, near_ref, far_ref)
        d_after = cot_ref[rows].astype(jnp.float32) + norm_back(
            after_ref[rows], d_second, gain_ref[...]
        )
        d_after_ref[rows] = d_after
        d_mix_ref[rows] = d_after.astype(jnp.bfloat16)
        return carry

    row_chunks(after_ref.shape[0], chunk)


def token_back_body(
    order_ref, tok_ref, d_after_ref, keep_ref, near_ref, far_ref, gain_ref, out_ref
):
    block = tok_ref.shape[1] // 8

    def chunk(rows, carry):
        d_first = summed_rows(rows, keep_ref, near_ref, far_ref)
        values = d_after_ref[rows] + norm_back(
            tok_ref[rows].astype(jnp.float32), d_first, gain_ref[...]
        )
        for b in range(8):
            there = pl.ds(pl.multiple_of(order_ref[b] * block, block), block)
            out_ref[rows, there] = values[:, b * block : b * block + block]
        return carry

    row_chunks(tok_ref.shape[0], chunk)


def piece_at(block, at):
    apart = block ^ at
    return (apart & 1) * 2 + (apart >> 1)


def head_lanes(columns, first, lanes):
    rows = columns.shape[0]
    even = jnp.broadcast_to(columns[:, first : first + 1], (rows, 128))
    odd = jnp.broadcast_to(columns[:, first + 1 : first + 2], (rows, 128))
    return jnp.where(lanes < HEAD, even, odd)


def lane_ids(rows, cols):
    return lax.broadcasted_iota(jnp.int32, (rows, cols), 1)


def row_ids(rows, cols):
    return lax.broadcasted_iota(jnp.int32, (rows, cols), 0)


def dot_nt(left_side, right_side, **kw):
    return lax.dot_general(
        left_side, right_side, (((1,), (1,)), ((), ())), preferred_element_type=jnp.float32, **kw
    )


def dot_nn(left_side, right_side):
    return jnp.dot(left_side, right_side, preferred_element_type=jnp.float32)


def dot_tn(left_side, right_side):
    return lax.dot_general(
        left_side, right_side, (((0,), (0,)), ((), ())), preferred_element_type=jnp.float32
    )


def conv_window(window, taps, offset, keep):
    rows = window.shape[0] - 8
    summed = window[8:] * taps[CONV - 1 : CONV] + offset
    for lag in range(1, CONV):
        summed = summed + window[8 - lag : 8 - lag + rows] * keep[:, lag : lag + 1] * (
            taps[CONV - 1 - lag : CONV - lag]
        )
    return summed


def log_one_plus(values):
    ratio = values / (2.0 + values)
    square = ratio * ratio
    series = jnp.full_like(values, 1.0 / 15.0)
    for odd in (13, 11, 9, 7, 5, 3, 1):
        series = series * square + 1.0 / odd
    return 2.0 * ratio * series


def scan_lanes(values, reverse):
    length = values.shape[1]
    lanes = lane_ids(*values.shape)
    step = 1
    while step < length:
        if reverse:
            moved = jnp.where(lanes < length - step, pltpu.roll(values, length - step, 1), 0.0)
        else:
            moved = jnp.where(lanes >= step, pltpu.roll(values, step, 1), 0.0)
        values = values + moved
        step = step * 2
    return values


def pair_mask(seg_col, seg_row, at_t, at_s):
    size = seg_col.shape[0]
    rows = row_ids(size, size) + at_t * size
    cols = lane_ids(size, size) + at_s * size
    return (seg_col == seg_row) & (rows >= cols)


def swap_halves(values, lanes):
    half = HEAD // 2
    return jnp.where(
        lanes % HEAD < half, pltpu.roll(values, 128 - half, 1), pltpu.roll(values, half, 1)
    )


def ssd_forward_body(
    heads,
    at_ref,
    proj_ref,
    segc_ref,
    segr_ref,
    keep_ref,
    taps_ref,
    tapb_ref,
    rate_ref,
    scan_ref,
    mixed_ref,
    raw_ref,
    pre_ref,
    basis_ref,
    inputs_ref,
    rows_ref,
    cols_ref,
    xpad,
    bpad,
    dtr,
):
    blocks, size = proj_ref.shape[0], proj_ref.shape[1]
    channels = mixed_ref.shape[1]
    states = basis_ref.shape[1]
    tail = proj_ref.shape[2] - states - 128
    at = at_ref[0]
    xpad[0:8] = jnp.zeros((8, channels), jnp.float32)
    bpad[0:8] = jnp.zeros((8, states), jnp.float32)

    def load(a, carry):
        rows = pl.ds(pl.multiple_of(a * size + 8, 8), size)
        block = piece_at(a, at)
        xpad[rows] = proj_ref[block, :, :channels]
        bpad[rows] = proj_ref[block, :, tail : tail + states]
        here = pl.ds(pl.multiple_of(a * size, size), size)
        raw_ref[here, :channels] = proj_ref[block, :, :channels].astype(jnp.bfloat16)
        raw_ref[here, channels:] = proj_ref[block, :, tail : tail + states].astype(jnp.bfloat16)
        steps = proj_ref[block, :, tail + states :]
        dtr[:, pl.ds(pl.multiple_of(a * size, size), size)] = steps.T[0:8]
        return carry

    lax.fori_loop(0, blocks, load, 0)
    raw = dtr[...] + rate_ref[:, 0:1]
    step_size = jnp.maximum(raw, 0.0) + log_one_plus(jnp.exp(-jnp.abs(raw)))
    log_rate = -step_size * jnp.exp(rate_ref[:, 1:2])
    cum = scan_lanes(log_rate, False) * LOG2_E
    length = raw.shape[1]
    rows_ref[0:8] = step_size
    rows_ref[8:16] = cum
    rows_ref[16:24] = raw
    cols_ref[...] = jnp.concatenate(
        [step_size, cum, jnp.zeros((112, length), jnp.float32)], axis=0
    ).T
    lanes = lane_ids(size, 128)

    def prepare_block(a, carry):
        window = pl.ds(pl.multiple_of(a * size, size), size + 8)
        rows = pl.ds(pl.multiple_of(a * size, size), size)
        keep = keep_ref[rows]
        columns = cols_ref[rows]
        bpre = conv_window(bpad[window], tapb_ref[0:4], tapb_ref[4:5], keep)
        pre_ref[rows, channels:] = bpre.astype(jnp.bfloat16)
        basis_ref[rows] = (bpre * jax.nn.sigmoid(bpre)).astype(jnp.bfloat16)
        for pair in range(channels // 128):
            span = slice(pair * 128, pair * 128 + 128)
            xpre = conv_window(xpad[window, span], taps_ref[0:4, span], taps_ref[4:5, span], keep)
            pre_ref[rows, span] = xpre.astype(jnp.bfloat16)
            mixed = (xpre * jax.nn.sigmoid(xpre)).astype(jnp.bfloat16)
            mixed_ref[rows, span] = mixed
            steps = head_lanes(columns, 2 * pair, lanes)
            inputs_ref[rows, span] = (steps * mixed.astype(jnp.float32)).astype(jnp.bfloat16)
        return carry

    lax.fori_loop(0, blocks, prepare_block, 0)
    state = states // 2

    def row_block(i, carry):
        rows_t = pl.ds(pl.multiple_of(i * size, size), size)
        basis_c = basis_ref[rows_t, state:]
        seg_t = segc_ref[rows_t]
        columns = cols_ref[rows_t]

        def pair_block(j, totals):
            rows_s = pl.ds(pl.multiple_of(j * size, size), size)
            allowed = pair_mask(seg_t, segr_ref[:, rows_s], i, j)
            gram = jnp.where(allowed, dot_nt(basis_c, basis_ref[rows_s, :state]), 0.0)
            cum_s = rows_ref[8:16, rows_s]
            fresh = []
            for pair in range(heads // 2):
                values = inputs_ref[rows_s, pair * 128 : pair * 128 + 128]
                outs = []
                for h in (2 * pair, 2 * pair + 1):
                    spread = columns[:, 8 + h : 9 + h] - cum_s[h : h + 1]
                    weights = (gram * jnp.exp2(jnp.minimum(spread, 0.0))).astype(jnp.bfloat16)
                    outs.append(dot_nn(weights, values))
                fresh.append(totals[pair] + jnp.where(lanes < HEAD, outs[0], outs[1]))
            return tuple(fresh)

        zero = jnp.zeros((size, 128), jnp.float32)
        totals = lax.fori_loop(0, i + 1, pair_block, (zero,) * (heads // 2))
        for pair in range(heads // 2):
            scan_ref[rows_t, pair * 128 : pair * 128 + 128] = totals[pair]
        return carry

    lax.fori_loop(0, blocks, row_block, 0)


def attend_forward_body(
    count,
    at_ref,
    first_ref,
    proj_ref,
    scan_ref,
    mixed_ref,
    segc_ref,
    segr_ref,
    cos_ref,
    sin_ref,
    gain_ref,
    *refs,
):
    parts = refs[:count]
    cat_ref, gate_ref, combined_ref, query_ref, keyk_ref, valv_ref, logs_ref = refs[count:-2]
    weight_ref, out_weight_ref = refs[-2:]
    wide = weight_ref.shape[1]
    stack_rows([part.at[:, :wide] for part in parts], weight_ref)
    stack_rows([part.at[:, wide:] for part in parts], out_weight_ref)
    blocks, size = proj_ref.shape[0], proj_ref.shape[1]
    channels = scan_ref.shape[1]
    at = at_ref[0]
    lanes = lane_ids(size, 128)
    half_type = jnp.bfloat16

    def finish_block(a, carry):
        rows = pl.ds(pl.multiple_of(a * size, size), size)
        block = piece_at(a, at)
        mine = dot_nn(first_ref[block], weight_ref[...])
        gate, query = mine[:, :channels], mine[:, channels:]
        gate_ref[block] = gate.astype(half_type)
        combined = scan_ref[rows] + gain_ref[1:2] * mixed_ref[rows].astype(jnp.float32)
        combined_ref[rows] = combined.astype(half_type)
        gated = combined * (gate * jax.nn.sigmoid(gate))
        inverse = lax.rsqrt(jnp.mean(gated * gated, axis=-1, keepdims=True) + EPS)
        cat_ref[block, :, :channels] = (gated * inverse * gain_ref[0:1]).astype(half_type)
        cosine, sine = cos_ref[rows], sin_ref[rows]
        query_ref[rows] = (query * cosine + swap_halves(query, lanes) * sine).astype(half_type)
        keyval = proj_ref[block, :, channels : channels + 128]
        keyval = keyval * jnp.where(lanes < HEAD, cosine, 1.0) + swap_halves(
            keyval, lanes
        ) * jnp.where(lanes < HEAD, sine, 0.0)
        moved = pltpu.roll(keyval, HEAD, 1)
        keyk_ref[rows] = jnp.where(lanes < HEAD, keyval, moved).astype(half_type)
        valv_ref[rows] = jnp.where(lanes < HEAD, moved, keyval).astype(half_type)
        return carry

    lax.fori_loop(0, blocks, finish_block, 0)
    for i in range(blocks):
        width = (i + 1) * size
        rows = slice(i * size, width)
        query = query_ref[rows]
        places = row_ids(size, width) + i * size
        allowed = (segc_ref[rows] == segr_ref[:, :width]) & (places >= lane_ids(size, width))
        outs, logs = [], []
        for h in range(2):
            mine = (lanes < HEAD) if h == 0 else (lanes >= HEAD)
            masked = jnp.where(mine, query, jnp.zeros_like(query))
            scores = dot_nt(masked, keyk_ref[:width]) * HEAD ** (-0.5)
            scores = jnp.where(allowed, scores, NEG_FILL)
            top = jnp.max(scores, axis=-1, keepdims=True)
            powers = jnp.exp(scores - top)
            total = jnp.sum(powers, axis=-1, keepdims=True)
            outs.append(dot_nn(powers.astype(half_type), valv_ref[:width]) / total)
            logs.append(top + jnp.log(total))
        cat_ref[piece_at(i, at), :, channels:] = jnp.where(lanes < HEAD, outs[0], outs[1]).astype(half_type)
        logs_ref[rows] = jnp.where(lanes < HEAD, logs[0], logs[1])


def gate_backward_body(
    at_ref,
    gate_ref,
    mine_ref,
    far_ref,
    near_ref,
    cross_ref,
    weight_ref,
    combined_ref,
    gain_ref,
    dgate_ref,
    dcomb_ref,
    small_ref,
    dmix_ref,
    datt_ref,
):
    blocks, size = gate_ref.shape[0], gate_ref.shape[1]
    channels = combined_ref.shape[1]
    at = at_ref[0]
    half_type = jnp.bfloat16
    for p, piece in enumerate((mine_ref, far_ref, near_ref, cross_ref)):
        dmix_ref[p] = piece[...]

    def finish_block(a, carry):
        grad_gain = carry
        rows = pl.ds(pl.multiple_of(a * size, size), size)
        block = piece_at(a, at)
        d_cat = dot_nn(dmix_ref[block], weight_ref[...])
        datt_ref[rows] = d_cat[:, channels:].astype(half_type)
        gate = gate_ref[block].astype(jnp.float32)
        sig = jax.nn.sigmoid(gate)
        act = gate * sig
        combined = combined_ref[rows].astype(jnp.float32)
        gated = combined * act
        inverse = lax.rsqrt(jnp.mean(gated * gated, axis=-1, keepdims=True) + EPS)
        normed = gated * inverse
        d_out = d_cat[:, :channels]
        grad_gain = grad_gain + jnp.sum(d_out * normed, axis=0, keepdims=True)
        scaled = d_out * gain_ref[0:1]
        d_gated = inverse * (scaled - normed * jnp.mean(scaled * normed, axis=-1, keepdims=True))
        d_comb = d_gated * act
        dcomb_ref[rows] = d_comb
        d_gate = d_gated * combined * sig * (1.0 + gate * (1.0 - sig))
        dgate_ref[block] = d_gate.astype(half_type)
        return grad_gain

    grad_gain = lax.fori_loop(0, blocks, finish_block, jnp.zeros((1, channels), jnp.float32))
    small_ref[...] = jnp.broadcast_to(grad_gain, small_ref.shape)


def attend_backward_body(
    at_ref,
    datt_ref,
    segc_ref,
    segr_ref,
    cos_ref,
    sin_ref,
    query_ref,
    keyk_ref,
    valv_ref,
    logs_ref,
    dproj_ref,
    dkey,
    dval,
):
    blocks, size = dproj_ref.shape[0], dproj_ref.shape[1]
    at = at_ref[0]
    lanes = lane_ids(size, 128)
    half_type = jnp.bfloat16
    dkey[...] = jnp.zeros_like(dkey)
    dval[...] = jnp.zeros_like(dval)
    for i in range(blocks):
        width = (i + 1) * size
        rows = slice(i * size, width)
        query = query_ref[rows]
        d_att = datt_ref[rows]
        logs = logs_ref[rows]
        places = row_ids(size, width) + i * size
        allowed = (segc_ref[rows] == segr_ref[:, :width]) & (places >= lane_ids(size, width))
        outs = []
        for h in range(2):
            mine = (lanes < HEAD) if h == 0 else (lanes >= HEAD)
            masked = jnp.where(mine, query, jnp.zeros_like(query))
            d_masked = jnp.where(mine, d_att, jnp.zeros_like(d_att))
            scores = dot_nt(masked, keyk_ref[:width]) * HEAD ** (-0.5)
            scores = jnp.where(allowed, scores, NEG_FILL)
            probs = jnp.exp(scores - logs[:, h * HEAD : h * HEAD + 1])
            d_probs = dot_nt(d_masked, valv_ref[:width])
            mean = jnp.sum(probs * d_probs, axis=-1, keepdims=True)
            d_scores = (probs * (d_probs - mean)).astype(half_type)
            outs.append(dot_nn(d_scores, keyk_ref[:width]))
            dkey[:width] += dot_tn(d_scores, masked)
            dval[:width] += dot_tn(probs.astype(half_type), d_masked)
        d_query = jnp.where(lanes < HEAD, outs[0], outs[1]) * HEAD ** (-0.5)
        cosine, sine = cos_ref[rows], sin_ref[rows]
        d_query = d_query * cosine - swap_halves(d_query, lanes) * sine
        dproj_ref[piece_at(i, at), :, :128] = d_query.astype(half_type)

    def key_block(a, carry):
        rows = pl.ds(pl.multiple_of(a * size, size), size)
        d_key, d_val = dkey[rows], dval[rows]
        d_key = (d_key + pltpu.roll(d_key, HEAD, 1)) * HEAD ** (-0.5)
        d_val = d_val + pltpu.roll(d_val, HEAD, 1)
        d_key = d_key * cos_ref[rows] - swap_halves(d_key, lanes) * sin_ref[rows]
        dproj_ref[piece_at(a, at), :, 128:] = jnp.where(lanes < HEAD, d_key, d_val).astype(
            half_type
        )
        return carry

    lax.fori_loop(0, blocks, key_block, 0)


def silu_slope(values):
    sig = jax.nn.sigmoid(values)
    return sig * (1.0 + values * (1.0 - sig))


def conv_back(d_window, keep_window, taps):
    rows = d_window.shape[0] - 8
    summed = d_window[:rows] * taps[CONV - 1 : CONV]
    for lag in range(1, CONV):
        moved = d_window * keep_window[:, lag : lag + 1]
        summed = summed + moved[lag : lag + rows] * taps[CONV - 1 - lag : CONV - lag]
    return summed


def conv_grads(d_pre, window, keep):
    rows = d_pre.shape[0]
    sums = []
    for tap in range(CONV):
        lag = CONV - 1 - tap
        moved = window[8 - lag : 8 - lag + rows]
        if lag:
            moved = moved * keep[:, lag : lag + 1]
        sums.append(jnp.sum(d_pre * moved, axis=0, keepdims=True))
    sums.append(jnp.sum(d_pre, axis=0, keepdims=True))
    sums.append(jnp.zeros((8 - len(sums), d_pre.shape[1]), jnp.float32))
    return jnp.concatenate(sums, axis=0)


def ssd_backward_body(
    heads,
    at_ref,
    dcomb_ref,
    scan_ref,
    segc_ref,
    segr_ref,
    mixed_ref,
    basis_ref,
    inputs_ref,
    rows_ref,
    cols_ref,
    dint,
    dbt,
    dcb,
    qrow,
    mixt,
    skip_ref,
    dsc,
    dst,
    cbt,
):
    length, channels = scan_ref.shape
    state = dbt.shape[0]
    size = length // 4
    blocks = 4
    half_type = jnp.bfloat16
    lanes = lane_ids(size, 128)
    dint[...] = jnp.zeros_like(dint)
    dbt[...] = jnp.zeros_like(dbt)
    head_of = jnp.where(
        lane_ids(8, channels) // HEAD == row_ids(8, channels), 1.0, 0.0
    ).astype(jnp.float32)

    def load(a, carry):
        rows = pl.ds(pl.multiple_of(a * size, size), size)
        d_comb = dcomb_ref[rows]
        d_scan = d_comb.astype(half_type)
        dsc[rows] = d_scan
        d_full = d_scan.astype(jnp.float32)
        dst[:, rows] = d_full.T.astype(half_type)
        cbt[:, rows] = basis_ref[rows, state:].astype(jnp.float32).T.astype(half_type)
        mixed = mixed_ref[rows].astype(jnp.float32)
        mixt[:, rows] = mixed.T
        qrow[:, rows] = dot_nt(head_of, d_full * scan_ref[rows], precision=lax.Precision.HIGHEST)
        return carry + jnp.sum(d_comb * mixed, axis=0, keepdims=True)

    skips = lax.fori_loop(0, blocks, load, jnp.zeros((1, channels), jnp.float32))
    skip_ref[...] = jnp.broadcast_to(skips, skip_ref.shape)

    def row_block(i, carry):
        rows_t = pl.ds(pl.multiple_of(i * size, size), size)
        basis_c = basis_ref[rows_t, state:]
        seg_t = segc_ref[rows_t]
        columns = cols_ref[rows_t]

        def pair_block(j, total):
            rows_s = pl.ds(pl.multiple_of(j * size, size), size)
            allowed = pair_mask(seg_t, segr_ref[:, rows_s], i, j)
            gram = jnp.where(allowed, dot_nt(basis_c, basis_ref[rows_s, :state]), 0.0)
            cum_s = rows_ref[8:16, rows_s]
            d_gram = jnp.zeros((size, size), jnp.float32)
            for pair in range(heads // 2):
                span = slice(pair * 128, pair * 128 + 128)
                values = inputs_ref[rows_s, span]
                d_scan = dsc[rows_t, span]
                for h in (2 * pair, 2 * pair + 1):
                    mine = (lanes < HEAD) if h % 2 == 0 else (lanes >= HEAD)
                    spread = columns[:, 8 + h : 9 + h] - cum_s[h : h + 1]
                    decay = jnp.exp2(jnp.minimum(spread, 0.0))
                    weights = (gram * decay).astype(half_type)
                    d_weights = dot_nt(jnp.where(mine, d_scan, jnp.zeros_like(d_scan)), values)
                    d_gram = d_gram + d_weights * decay
                    chans = slice(h * HEAD, h * HEAD + HEAD)
                    dint[chans, rows_s] += dot_nn(dst[chans, rows_t], weights)
            d_gram = jnp.where(allowed, d_gram, 0.0).astype(half_type)
            dbt[:, rows_s] += dot_nn(cbt[:, rows_t], d_gram)
            return total + dot_nn(d_gram, basis_ref[rows_s, :state])

        dcb[rows_t] = lax.fori_loop(0, i + 1, pair_block, jnp.zeros((size, state), jnp.float32))
        return carry

    lax.fori_loop(0, blocks, row_block, 0)


def conv_backward_body(
    heads,
    at_ref,
    raw_ref,
    dcomb_ref,
    keep_ref,
    taps_ref,
    tapb_ref,
    rate_ref,
    gain_ref,
    pre_ref,
    rows_ref,
    dint_ref,
    dbt,
    dcb,
    qrow_ref,
    mixt,
    dproj_ref,
    gradx_ref,
    gradb_ref,
    grads_ref,
    xpad,
    bpad,
    dpx,
    dpb,
    dint,
    qrow,
):
    blocks, size = dproj_ref.shape[0], dproj_ref.shape[1]
    channels = dcomb_ref.shape[1]
    states = pre_ref.shape[1] - channels
    length = blocks * size
    at = at_ref[0]
    half_type = jnp.bfloat16
    xpad[0:8] = jnp.zeros((8, channels), jnp.float32)
    bpad[0:8] = jnp.zeros((8, states), jnp.float32)
    dpx[length : length + 8] = jnp.zeros((8, channels), jnp.float32)
    dpb[length : length + 8] = jnp.zeros((8, states), jnp.float32)

    def load(a, carry):
        padded = pl.ds(pl.multiple_of(a * size + 8, 8), size)
        rows = pl.ds(pl.multiple_of(a * size, size), size)
        xpad[padded] = raw_ref[rows, :channels].astype(jnp.float32)
        bpad[padded] = raw_ref[rows, channels:].astype(jnp.float32)
        return carry

    lax.fori_loop(0, blocks, load, 0)
    step_size = rows_ref[0:8]
    raw = rows_ref[16:24]
    d_step, col_part = [], []
    for h in range(heads):
        chans = slice(h * HEAD, h * HEAD + HEAD)
        d_inputs = dint_ref[chans]
        mixed = mixt[chans]
        scaled = step_size[h : h + 1] * mixed
        d_step.append(jnp.sum(d_inputs * mixed, axis=0, keepdims=True))
        inputs = scaled.astype(half_type).astype(jnp.float32)
        col_part.append(jnp.sum(d_inputs * inputs, axis=0, keepdims=True))
        dint[chans] = d_inputs * step_size[h : h + 1]
    blank = jnp.zeros((8 - heads, length), jnp.float32)
    d_step = jnp.concatenate(d_step + [blank], axis=0)
    d_cum = qrow_ref[...] - jnp.concatenate(col_part + [blank], axis=0)
    d_log = scan_lanes(d_cum, True)
    rate = jnp.exp(rate_ref[:, 1:2])
    grad_rate = jnp.sum(d_log * (-step_size * rate), axis=1, keepdims=True)
    d_raw = (d_step - d_log * rate) * jax.nn.sigmoid(raw)
    d_raw = jnp.where(row_ids(8, length) < heads, d_raw, 0.0)
    grad_bias = jnp.sum(d_raw, axis=1, keepdims=True)
    lanes8 = lane_ids(8, 128)
    grads_ref[...] = jnp.where(lanes8 == 0, grad_bias, jnp.where(lanes8 == 1, grad_rate, 0.0))
    qrow[...] = d_raw

    def grad_block(a, carry):
        rows = pl.ds(pl.multiple_of(a * size, size), size)
        d_mixed = dint[:, rows].T + dcomb_ref[rows] * gain_ref[1:2]
        dpx[rows] = d_mixed * silu_slope(pre_ref[rows, :channels].astype(jnp.float32))
        d_basis = jnp.concatenate([dbt[:, rows].T, dcb[rows]], axis=1)
        dpb[rows] = d_basis * silu_slope(pre_ref[rows, channels:].astype(jnp.float32))
        return carry

    lax.fori_loop(0, blocks, grad_block, 0)

    def conv_block(a, carry):
        grad_x, grad_b = carry
        rows = pl.ds(pl.multiple_of(a * size, size), size)
        window = pl.ds(pl.multiple_of(a * size, size), size + 8)
        block = piece_at(a, at)
        keep_window = keep_ref[window]
        keep = keep_window[:size]
        d_wide = dpx[window]
        dproj_ref[block, :, :channels] = conv_back(d_wide, keep_window, taps_ref[...]).astype(
            half_type
        )
        grad_x = grad_x + conv_grads(d_wide[:size], xpad[window], keep)
        d_wide = dpb[window]
        dproj_ref[block, :, channels : channels + states] = conv_back(
            d_wide, keep_window, tapb_ref[...]
        ).astype(half_type)
        grad_b = grad_b + conv_grads(d_wide[:size], bpad[window], keep)
        d_steps = jnp.concatenate([qrow[:, rows], jnp.zeros((120, size), jnp.float32)], axis=0)
        dproj_ref[block, :, channels + states :] = d_steps.T.astype(half_type)
        return grad_x, grad_b

    grad_x, grad_b = lax.fori_loop(
        0,
        blocks,
        conv_block,
        (jnp.zeros((8, channels), jnp.float32), jnp.zeros((8, states), jnp.float32)),
    )
    gradx_ref[...] = grad_x
    gradb_ref[...] = grad_b


def stack_rows(pieces, out_ref):
    begin_at = 0
    for piece in pieces:
        out_ref[begin_at : begin_at + piece.shape[0]] = piece[...]
        begin_at = begin_at + piece.shape[0]


def project_body(count, order_ref, *refs):
    pieces, parts = refs[:4], refs[4 : 4 + count]
    first_ref, proj_ref, weight_ref, small_ref, taps_ref = refs[4 + count :]
    width = weight_ref.shape[0]
    rows = proj_ref.shape[1]
    states = taps_ref.shape[1]
    stack_rows(parts, weight_ref)
    small = weight_ref[:, weight_ref.shape[1] - 128 :].astype(jnp.float32).T[8:16]
    small_ref[...] = small
    gain = small[0:1]
    for p, piece in enumerate(pieces):
        first = (piece[...].astype(jnp.float32) * gain).astype(jnp.bfloat16)
        first_ref[p] = first
        proj_ref[p] = dot_nn(first, weight_ref[...])
    feature = row_ids(width, states)
    block = width // 8
    place = feature % block
    for b in range(8):
        place = place + jnp.where(feature // block == b, order_ref[b] * block, 0)
    channel = lane_ids(width, states)
    taps = []
    for k in range(CONV + 1):
        picked = jnp.where(place == channel * CONV + k % CONV, 1.0, 0.0).astype(jnp.bfloat16)
        found = dot_nn(small.astype(jnp.bfloat16), picked)
        taps.append(found[2:3] if k < CONV else found[3:4])
    taps.append(jnp.zeros((8 - len(taps), states), jnp.float32))
    taps_ref[...] = jnp.concatenate(taps, axis=0)


def product_body(_, values_ref, weight_ref, keep_ref, give_ref):
    rows = values_ref.shape[1]
    columns = slice(weight_ref.shape[1] - values_ref.shape[2], None)
    for p in (3, 1, 2, 0):
        result = dot_nt(values_ref[p], weight_ref[:, columns])
        if p < 2:
            keep_ref[p * rows : p * rows + rows] = result
        else:
            give_ref[p * rows - 2 * rows : p * rows - rows] = result.astype(jnp.bfloat16)


def first_back_body(
    _, gate_ref, attn_ref, scan_ref, late_ref, weight_ref, keep_ref, give_ref, token_ref
):
    token_ref[...] = jnp.zeros_like(token_ref)
    rows, channels = gate_ref.shape[1], gate_ref.shape[2]
    wide = channels + 128
    for p in (3, 2, 1, 0):
        result = dot_nt(gate_ref[p], late_ref[:, :channels])
        result = result + dot_nt(attn_ref[p, :, :128], late_ref[:, channels:wide])
        result = result + dot_nt(attn_ref[p, :, 128:], weight_ref[:, channels:wide])
        result = result + dot_nt(scan_ref[p, :, :channels], weight_ref[:, :channels])
        result = result + dot_nt(scan_ref[p, :, channels:], weight_ref[:, wide:])
        if p < 2:
            keep_ref[p * rows : p * rows + rows] = result
        else:
            give_ref[p * rows - 2 * rows : p * rows - rows] = result.astype(jnp.bfloat16)


def ffn_body(slots, fresh, _, *refs):
    pieces, cots = refs[0:2], refs[2:4]
    if fresh:
        parts, outs = refs[4:-7], refs[-7:]
        weight_ref = outs[6]
        stack_rows(parts, weight_ref)
    else:
        weight_ref, outs = refs[4], refs[-6:]
    second_ref, cot_ref, hidden_ref, dgu_ref, dkeep, dgive = outs[:6]
    hidden_local = hidden_ref.shape[2]
    rows = second_ref.shape[1]
    gate_up_weight = weight_ref.at[:, : 2 * hidden_local]
    down_weight = weight_ref.at[:, 2 * hidden_local :]
    for p, piece, cots_ref in zip(slots, pieces, cots):
        values, cot = piece[...], cots_ref[...]
        second_ref[p] = values
        cot_ref[p] = cot
        gate_up = dot_nn(values, gate_up_weight[...])
        d_hidden = dot_nn(cot, down_weight[...])
        gate, up = gate_up[:, :hidden_local], gate_up[:, hidden_local:]
        sig = jax.nn.sigmoid(gate)
        act = gate * sig
        hidden = (act * up).astype(jnp.bfloat16)
        hidden_ref[p] = hidden
        d_gate = (d_hidden * up * sig * (1.0 + gate * (1.0 - sig))).astype(jnp.bfloat16)
        d_up = (d_hidden * act).astype(jnp.bfloat16)
        dgu_ref[p, :, :hidden_local] = d_gate
        dgu_ref[p, :, hidden_local:] = d_up
        d_second = dot_nt(dgu_ref[p], gate_up_weight[...])
        if p < 2:
            dkeep[...] = d_second
        else:
            dgive[...] = d_second.astype(jnp.bfloat16)


def pick_rows(values, block, rows):
    picked = jnp.zeros((rows, values.shape[1]), values.dtype)
    for g in range(values.shape[0] // rows):
        picked = jnp.where(block == g, values[g * rows : g * rows + rows], picked)
    return picked


def shared_sums_body(conv_rows, at_ref, bc_ref, keyval_ref, *refs):
    *sums, ffn_ref, small_ref, keep_ref, give_ref = refs
    at, place = at_ref[0], at_ref[1]
    rows = keep_ref.shape[0] // 2
    states = bc_ref.shape[1]
    size = 4 * rows
    lanes = lane_ids(size, 128)
    by_row = sum(ref[...] for ref in sums)
    small = jnp.concatenate(
        [
            jnp.zeros((8, states), jnp.float32),
            small_ref[:, :states],
            jnp.zeros((112, states), jnp.float32),
        ],
        axis=0,
    ).T
    spot = row_ids(size, states)
    channel = (place * 4 + spot // rows) * conv_rows + spot % rows
    chosen = (channel == lane_ids(size, states)) & (spot % rows < conv_rows)
    small = jnp.dot(
        jnp.where(chosen, 1.0, 0.0),
        small,
        precision=lax.Precision.HIGHEST,
        preferred_element_type=jnp.float32,
    )
    gains = jnp.where(lanes == 0, by_row, jnp.where(lanes == 1, ffn_ref[...], small))
    values = jnp.concatenate([bc_ref[...], keyval_ref[...], gains], axis=1)
    for k in range(2):
        keep_ref[k * rows : k * rows + rows] = pick_rows(values, at ^ (2 * k), rows)
        give_ref[k * rows : k * rows + rows] = pick_rows(values, at ^ (2 * k + 1), rows)


def shared_total_body(at_ref, keep_ref, near_ref, far_ref, gains_ref, bc_ref, keyval_ref, out_ref):
    rows = far_ref.shape[0]
    states = bc_ref.shape[1]
    lanes = lane_ids(rows, 128)
    chip, other = keep_ref[:rows] + near_ref[:rows], far_ref[...]
    total = chip + other
    bc_ref[...] = total[:, :states]
    heads = [side[:, states : states + 128] for side in (chip, other)]
    low, high = [
        [jnp.where(at_ref[0] < 2, heads[k], heads[1 - k]) for k in range(2)][k] for k in range(2)
    ]
    keyval_ref[:, :128] = jnp.where(lanes < HEAD, low, pltpu.roll(high, HEAD, 1))
    keyval_ref[:, 128:] = jnp.where(lanes < HEAD, pltpu.roll(low, HEAD, 1), high)
    rounded = gains_ref[...].astype(jnp.bfloat16).astype(jnp.float32)
    out_ref[...] = total[:, states + 128 :] / rounded


def pack_body(turned, _, *refs):
    out_ref = refs[-1]
    begin_at = 0
    for index, ref in enumerate(refs[:-1]):
        values = ref[...]
        if index in turned:
            values = values.T
        out_ref[:, begin_at : begin_at + values.shape[1]] = values.astype(jnp.bfloat16)
        begin_at = begin_at + values.shape[1]


def shared_body(at_ref, mine_ref, near_ref, far_ref, cross_ref, step_ref, out_ref):
    at = at_ref[0]
    rows = mine_ref.shape[0]
    lanes = lane_ids(rows, 128)
    states = mine_ref.shape[1] - 384
    for j, ref in enumerate((mine_ref, near_ref, far_ref, cross_ref)):
        values = ref[...].astype(jnp.float32)
        here = pl.ds(pl.multiple_of((at ^ j) * rows, rows), rows)
        key, value = values[:, :128], values[:, 128:256]
        low = jnp.where(lanes < HEAD, key, pltpu.roll(value, HEAD, 1))
        high = jnp.where(lanes < HEAD, pltpu.roll(key, HEAD, 1), value)
        out_ref[here, :128] = jnp.where(at < 2, low, high).astype(jnp.bfloat16)
        out_ref[here, 128 : 128 + states] = values[:, 256 : 256 + states].astype(jnp.bfloat16)
        out_ref[here, 128 + states :] = (
            values[:, 256 + states :] + step_ref[here]
        ).astype(jnp.bfloat16)


def call_kernel(body, outs, scratch, *args, deps=(), micros=2, limit=8, aliases=None, distant=0, sems=0):
    shapes = [jax.ShapeDtypeStruct(shape, kind) for shape, kind in outs]
    count, extra = len(args), len(deps)
    whole = pl.BlockSpec(memory_space=pltpu.VMEM)

    def wrapped(*refs):
        body(*refs[:count], *refs[count + extra :])

    return pl.pallas_call(
        wrapped,
        out_shape=shapes,
        in_specs=[pl.BlockSpec(memory_space=pltpu.SMEM)]
        + [whole] * (count - 1 - distant)
        + [pl.BlockSpec(memory_space=pltpu.HBM)] * distant
        + [whole] * extra,
        out_specs=[whole] * len(shapes),
        scratch_shapes=[pltpu.VMEM(shape, kind) for shape, kind in scratch]
        + ([pltpu.SemaphoreType.DMA((sems,))] if sems else []),
        input_output_aliases=aliases or {},
        compiler_params=pltpu.CompilerParams(vmem_limit_bytes=limit * 2**20),
        cost_estimate=pl.CostEstimate(
            flops=int(micros * 1e9), bytes_accessed=0, transcendentals=0
        ),
    )(*args, *deps)


def sequence_tables(seg_ids):
    length = seg_ids.shape[0]
    places = jnp.arange(length, dtype=jnp.int32)
    starts = jnp.where((places == 0) | (seg_ids != jnp.roll(seg_ids, 1)), places, 0)
    position = places - lax.cummax(starts, axis=0)
    half_dim = HEAD // 2
    frequency = jnp.exp(-jnp.log(ROPE_BASE) * jnp.arange(half_dim, dtype=jnp.float32) / half_dim)
    angles = position.astype(jnp.float32)[:, None] * frequency[None, :]
    cosine, sine = jnp.cos(angles), jnp.sin(angles)
    cosine = jnp.concatenate([cosine] * 4, axis=1)
    sine = jnp.concatenate([-sine, sine] * 2, axis=1)
    masks = [jnp.ones((length,), jnp.float32)]
    for lag in range(1, CONV):
        masks.append(
            ((places >= lag) & (seg_ids == jnp.roll(seg_ids, lag))).astype(jnp.float32)
        )
    masks = jnp.stack(masks + [jnp.zeros((length,), jnp.float32)] * (8 - CONV), axis=1)
    return cosine, sine, jnp.pad(masks, ((0, 8), (0, 0)))


def tap_rows(kernel, offset):
    taps = jnp.concatenate([kernel.T, offset[None, :]], axis=0)
    return jnp.pad(taps, ((0, 8 - taps.shape[0]), (0, 0)))


def shards(
    tokens,
    segment_ids,
    cotangent,
    norm_gain,
    w_z,
    w_x,
    w_bc,
    w_dt,
    conv_x,
    conv_bias_x,
    conv_bc,
    conv_bias_bc,
    dt_bias,
    a_log,
    d_skip,
    mixer_gain,
    w_mixer_out,
    w_query,
    w_keyval,
    w_attn_out,
    ffn_gain,
    w_gate,
    w_up,
    w_down,
):
    half_type = jnp.bfloat16
    full_type = jnp.float32
    rows, width = tokens.shape
    length = segment_ids.shape[0]
    channels = w_z.shape[1]
    heads = w_dt.shape[1]
    hidden_local = w_gate.shape[1]
    states = 2 * STATE
    blocks = length // rows

    row_count = w_bc.shape[0]
    gain_rows = norm_gain.shape[0]
    conv_rows = conv_bc.shape[0]
    at = lax.axis_index("tp").astype(jnp.int32).reshape(1)
    order = feature_order()
    x_at, core_at = place_bits()
    x_core = jnp.zeros((1,), jnp.int32)

    row_half = ((rows, width), half_type)
    row_full = ((rows, width), full_type)
    normed_mine, tok_rows, cot_mine = call_kernel(
        front_body, [row_half, row_half, row_half], [], order, tokens, cotangent
    )

    small = jnp.stack([norm_gain, ffn_gain, conv_bc.reshape(-1), jnp.repeat(conv_bias_bc, CONV)], 1)
    shared_in = jnp.concatenate(
        [w_keyval, w_bc, jnp.pad(small, ((0, 0), (8, 116)))], axis=1
    ).astype(half_type)
    step_wide = jnp.pad(w_dt, ((0, 0), (0, 128 - heads)))
    if staged():
        mine, far, near, cross = gather_pieces(shared_in)
        (shared_shard,) = call_kernel(
            shared_body,
            [((4 * row_count, states + 256), half_type)],
            [],
            at,
            mine,
            near,
            far,
            cross,
            step_wide,
            deps=[normed_mine],
            micros=1,
        )
    else:
        shared_all = lax.all_gather(shared_in, "tp", axis=0, tiled=True)
        key_rows, value_rows = (
            jnp.where(x_at == 0, shared_all[:, k : k + HEAD], shared_all[:, k + HEAD : k + 2 * HEAD])
            for k in (0, 128)
        )
        shared_shard = jnp.concatenate(
            [
                key_rows,
                value_rows,
                shared_all[:, 256 : 256 + states],
                shared_all[:, 256 + states :] + step_wide.astype(half_type),
            ],
            axis=1,
        )
    def pack(turned, *shards, deps=()):
        width_all = sum(shard.size for shard in shards) // w_x.shape[0]
        return call_kernel(
            functools.partial(pack_body, turned),
            [((w_x.shape[0], width_all), half_type)],
            [],
            x_core,
            *shards,
            deps=deps,
            micros=1,
        )[0]

    gather = Gather(jnp.concatenate([w_x.astype(half_type), shared_shard], axis=1))
    normed = gather_pieces(after(normed_mine, shared_shard))
    late_gather = Gather(
        pack((2, 3), w_z, w_query, w_mixer_out, w_attn_out, deps=[shared_shard, normed[2]])
    )
    seg_ids = after(segment_ids.reshape(-1, 128), shared_shard).reshape(-1)
    cosine, sine, keep_masks = sequence_tables(seg_ids)
    seg_col, seg_row = seg_ids[:, None], seg_ids[None, :]
    taps_x = tap_rows(conv_x, conv_bias_x)
    rates = jnp.pad(jnp.stack([dt_bias, a_log], axis=1), ((0, 8 - heads), (0, 126)))
    gains = jnp.stack([mixer_gain, jnp.repeat(d_skip, channels // heads)])
    gains = jnp.pad(gains, ((0, 6), (0, 0)))

    keep_masks = after(keep_masks, shared_shard)
    tables = [cosine, sine, keep_masks, taps_x, rates, gains]
    for k in range(3):
        gather.step(*(tables if k == 2 else []))
        late_step = late_gather.step()
    steps = gather.step()
    late_last = late_gather.step()
    ffn_shard = pack((2,), w_gate, w_up, w_down, deps=[*late_step[:1], *steps[1:]])
    ffn_gather = Gather(ffn_shard)

    parts = gather.parts()
    columns = channels + 128 + states + 128
    first_in, proj, weight, small_rows, taps_bc = call_kernel(
        functools.partial(project_body, len(parts)),
        [
            ((blocks, rows, width), half_type),
            ((blocks, rows, columns), full_type),
            ((width, columns), half_type),
            ((8, width), full_type),
            ((8, states), full_type),
        ],
        [],
        order,
        *normed,
        *parts,
        micros=6,
        limit=12,
    )
    gain_one, gain_two = small_rows[0:1], small_rows[1:2]

    ffn_gather.step(small_rows)
    cot = gather_pieces(after(cot_mine, small_rows))
    scan_out, mixed, raw, pre, basis, inputs, time_rows, time_cols = call_kernel(
        functools.partial(ssd_forward_body, heads),
        [
            ((length, channels), full_type),
            ((length, channels), half_type),
            ((length, channels + states), half_type),
            ((length, channels + states), half_type),
            ((length, states), half_type),
            ((length, channels), half_type),
            ((24, length), full_type),
            ((length, 128), full_type),
        ],
        [
            ((length + 8, channels), full_type),
            ((length + 8, states), full_type),
            ((8, length), full_type),
        ],
        at,
        proj,
        seg_col,
        seg_row,
        keep_masks,
        taps_x,
        taps_bc,
        rates,
        deps=[ffn_shard, late_gather.ready],
        micros=11,
        limit=12,
    )
    parts = late_gather.parts()
    head_half = ((length, 128), half_type)
    head_full = ((length, 128), full_type)
    ffn_gather.step(time_rows, *late_last[1:])
    cat, gate_in, combined, query, keyk, valv, logs, late_weight, out_weight = call_kernel(
        functools.partial(attend_forward_body, len(parts)),
        [
            ((blocks, rows, channels + 128), half_type),
            ((blocks, rows, channels), half_type),
            ((length, channels), half_type),
            head_half,
            head_half,
            head_half,
            head_full,
            ((width, channels + 128), half_type),
            ((width, channels + 128), half_type),
        ],
        [],
        at,
        first_in,
        proj,
        scan_out,
        mixed,
        seg_col,
        seg_row,
        cosine,
        sine,
        gains,
        *parts,
        deps=[ffn_gather.ready, cot[1]],
        micros=9,
        limit=12,
    )

    def row_products(values, weight, deps=()):
        return call_kernel(
            product_body,
            [((2 * rows, width), full_type), ((2 * rows, width), half_type)],
            [],
            x_core,
            values,
            weight,
            deps=deps,
        )

    keep, give = row_products(cat, out_weight, deps=ffn_gather.arrivals)
    ffn_gather.step(query)
    mix_terms = reduce_pieces(keep, give, ffn_gather.ready)
    ffn_gather.step()
    after_mix, second_mine = call_kernel(
        mixed_body,
        [row_full, row_half],
        [],
        order,
        tok_rows,
        *mix_terms[:3],
        gain_two,
        deps=[ffn_gather.ready],
    )
    second_far = flip(second_mine, "tp", 2)
    second_near = flip(second_mine, "tp", 1)

    parts = ffn_gather.parts()
    filled = [
        ((blocks, rows, width), half_type),
        ((blocks, rows, width), half_type),
        ((blocks, rows, hidden_local), half_type),
        ((blocks, rows, 2 * hidden_local), half_type),
    ]
    sums = [row_full, row_half]
    *filled_in, d_keep, d_give, ffn_weight = call_kernel(
        functools.partial(ffn_body, (0, 2), True),
        filled + sums + [((width, 3 * hidden_local), half_type)],
        [],
        x_core,
        second_mine,
        second_near,
        cot[0],
        cot[2],
        *parts,
        micros=5,
        limit=12,
    )
    *filled_in, d_keep_x, d_give_x = call_kernel(
        functools.partial(ffn_body, (1, 3), False),
        filled + sums,
        [],
        x_core,
        second_far,
        flip(after(second_far, d_give), "tp", 1),
        cot[1],
        cot[3],
        ffn_weight,
        *filled_in,
        micros=5,
        limit=12,
        aliases={6: 0, 7: 1, 8: 2, 9: 3},
    )
    second_in, cot_all, hidden, d_gate_up = (
        array.reshape(length, array.shape[2]) for array in filled_in
    )
    near = flip(d_give, "tp", 1)
    passed = d_keep_x + flip(d_give_x, "tp", 1).astype(full_type)
    d_second = d_keep, near, flip(passed.astype(half_type), "tp", 2)
    ffn_scatter = Scatter(
        [
            contract_rows(second_in, d_gate_up).astype(half_type),
            contract_rows(cot_all, hidden).astype(half_type),
        ],
    )

    d_after, d_mix = call_kernel(
        after_back_body,
        [row_full, row_half],
        [],
        order,
        after_mix,
        cot_mine,
        *d_second,
        gain_two,
        deps=ffn_scatter.arrivals,
    )
    ffn_scatter.step(3)
    d_mix_all = gather_pieces(d_mix, *ffn_scatter.arrivals)

    ffn_scatter.step(2)
    d_gate, d_comb, sums_gain, d_mix_whole, d_att = call_kernel(
        gate_backward_body,
        [
            ((blocks, rows, channels), half_type),
            ((length, channels), full_type),
            ((8, channels), full_type),
            ((blocks, rows, width), half_type),
            head_half,
        ],
        [],
        at,
        gate_in,
        *d_mix_all,
        out_weight,
        combined,
        gains,
        deps=[ffn_scatter.ready],
        micros=4,
    )
    (d_attn,) = call_kernel(
        attend_backward_body,
        [((blocks, rows, 256), half_type)],
        [((length, 128), full_type), ((length, 128), full_type)],
        at,
        d_att,
        seg_col,
        seg_row,
        cosine,
        sine,
        query,
        keyk,
        valv,
        logs,
        micros=7,
    )
    out_terms = reduce_pieces(*row_products(filled_in[2], ffn_weight, deps=[sums_gain]))
    first_rows = first_in.reshape(length, width)
    gate_scatter = Scatter(
        [
            contract_rows(first_rows, d_gate.reshape(length, channels)).astype(half_type),
            contract_rows(first_rows, d_attn.reshape(length, 256)).astype(half_type),
            contract_rows(
                d_mix_whole.reshape(length, width), cat.reshape(length, channels + 128)
            ).astype(half_type),
        ],
    )
    ffn_scatter.step(1, d_attn)
    d_inputs_t, d_basis_b, d_basis_c, q_rows, mixed_t, sums_skip = call_kernel(
        functools.partial(ssd_backward_body, heads),
        [
            ((channels, length), full_type),
            ((STATE, length), full_type),
            ((length, STATE), full_type),
            ((8, length), full_type),
            ((channels, length), full_type),
            ((8, channels), full_type),
        ],
        [
            ((length, channels), half_type),
            ((channels, length), half_type),
            ((STATE, length), half_type),
        ],
        at,
        d_comb,
        scan_out,
        seg_col,
        seg_row,
        mixed,
        basis,
        inputs,
        time_rows,
        time_cols,
        deps=[ffn_scatter.ready, gate_scatter.ready, out_terms[3]],
        micros=12,
        limit=12,
    )
    gate_scatter.step(3, sums_skip)
    d_scan, sums_x, sums_bc, sums_rate = call_kernel(
        functools.partial(conv_backward_body, heads),
        [
            ((blocks, rows, channels + states + 128), half_type),
            ((8, channels), full_type),
            ((8, states), full_type),
            ((8, 128), full_type),
        ],
        [
            ((length + 8, channels), full_type),
            ((length + 8, states), full_type),
            ((length + 8, channels), full_type),
            ((length + 8, states), full_type),
            ((channels, length), full_type),
            ((8, length), full_type),
        ],
        at,
        raw,
        d_comb,
        keep_masks,
        taps_x,
        taps_bc,
        rates,
        gains,
        pre,
        time_rows,
        d_inputs_t,
        d_basis_b,
        d_basis_c,
        q_rows,
        mixed_t,
        deps=[gate_scatter.ready, out_terms[2], *ffn_scatter.arrivals],
        micros=7,
        limit=14,
    )
    smalls = join_columns([sums_bc, sums_x, sums_gain, sums_skip, sums_rate])
    scan_scatter = Scatter(
        [
            contract_rows(
                first_rows, d_scan.reshape(length, channels + states + 128)
            ).astype(half_type)
        ],
        extra=smalls,
    )
    keep, give, token = call_kernel(
        first_back_body,
        [
            ((2 * rows, width), full_type),
            ((2 * rows, width), half_type),
            ((8, 128), full_type),
        ],
        [],
        x_core,
        d_gate,
        d_attn,
        d_scan,
        late_weight,
        weight,
        deps=[*scan_scatter.arrivals, *gate_scatter.arrivals],
        micros=4,
    )
    d_first = reduce_pieces(keep, give)
    scan_scatter.step(3, token)
    gate_scatter.step(2, d_first[3])
    scan_scatter.step(2, d_first[3])
    gate_scatter.step(1)
    scan_scatter.step(1, d_first[2])
    scan_ready = scan_scatter.ready
    sum_gate, sum_up, sum_down, ffn_rows = ffn_scatter.total(
        (
            (0, hidden_local, False),
            (hidden_local, hidden_local, False),
            (2 * hidden_local, hidden_local, True),
        ),
        ((0, 0, hidden_local), (hidden_local, 0, hidden_local)),
        w_gate,
        w_up,
        deps=[d_first[2]],
    )
    (grad_tokens,) = call_kernel(
        token_back_body,
        [row_full],
        [],
        order,
        tok_rows,
        d_after,
        *d_first[:3],
        gain_one,
        deps=[scan_ready],
    )

    sum_z, sum_mixer_out, sum_attn_out, sum_query, sum_keyval, gate_rows = gate_scatter.total(
        (
            (0, channels, False),
            (channels + 256, channels, True),
            (2 * channels + 256, 128, True),
            (channels, 128, False),
            (channels + 128, 128, False),
        ),
        ((0, 0, channels), (channels, 0, 128), (channels + 128, 0, 128)),
        w_z,
        w_query,
        shared_shard,
    )
    sum_x, sum_bc, sum_step, scan_rows, flat = scan_scatter.total(
        ((0, channels, False), (channels, states, False), (channels + states, heads, False)),
        ((0, 0, channels), (channels, 128, states), (channels + states, 0, heads)),
        w_x,
        shared_shard,
        w_dt,
    )
    keep, give = call_kernel(
        functools.partial(shared_sums_body, conv_rows),
        [((2 * row_count, states + 256), full_type)] * 2,
        [],
        jnp.concatenate([at, lax.axis_index("fsdp").astype(jnp.int32).reshape(1)]),
        sum_bc,
        sum_keyval,
        gate_rows,
        scan_rows,
        ffn_rows,
        flat,
        deps=[grad_tokens],
        micros=1,
    )
    near = flip(give, "tp", 1)
    far = flip(keep[row_count:] + near[row_count:], "tp", 2)
    grad_bc, grad_keyval, gain_sums = call_kernel(
        shared_total_body,
        [
            ((row_count, states), full_type),
            ((row_count, 256), full_type),
            ((row_count, 128), full_type),
        ],
        [],
        at,
        keep,
        near,
        far,
        jnp.pad(jnp.stack([norm_gain, ffn_gain], 1), ((0, 0), (0, 126)), constant_values=1.0),
        micros=1,
    )
    sum_gain_one, sum_gain_two = gain_sums[:, 0], gain_sums[:, 1]
    sum_conv, sum_bias = gain_sums[:conv_rows, 8:12], gain_sums[:conv_rows, 12]

    (layer_out,) = call_kernel(
        output_body,
        [row_half],
        [],
        order,
        after_mix,
        *out_terms[:3],
        deps=[d_first[3]],
    )
    x_sums = flat[:, states : states + channels]
    mixer_sums = flat[0, states + channels : states + 2 * channels]
    skip_sums = flat[0, states + 2 * channels : states + 3 * channels]
    rate_sums = flat[:, states + 3 * channels :]
    return (
        layer_out,
        grad_tokens,
        sum_gain_one,
        sum_z,
        sum_x,
        grad_bc,
        sum_step,
        x_sums[:4].T,
        x_sums[4],
        sum_conv,
        sum_bias,
        rate_sums[:heads, 0],
        rate_sums[:heads, 1],
        skip_sums.reshape(heads, channels // heads).sum(axis=1),
        mixer_sums,
        sum_mixer_out,
        sum_query,
        grad_keyval,
        sum_attn_out,
        sum_gain_two,
        sum_gate,
        sum_up,
        sum_down,
    )


def solution(mesh):
    placed = (
        P(("fsdp", "tp"), None),
        P("fsdp"),
        P(("fsdp", "tp"), None),
        P(("fsdp", "tp")),
        P("fsdp", "tp"),
        P("fsdp", "tp"),
        P(("fsdp", "tp"), None),
        P("fsdp", "tp"),
        P("tp", None),
        P("tp"),
        P(("fsdp", "tp"), None),
        P(("fsdp", "tp")),
        P("tp"),
        P("tp"),
        P("tp"),
        P("tp"),
        P("tp", "fsdp"),
        P("fsdp", "tp"),
        P(("fsdp", "tp"), None),
        P("tp", "fsdp"),
        P(("fsdp", "tp")),
        P("fsdp", "tp"),
        P("fsdp", "tp"),
        P("tp", "fsdp"),
    )
    return jax.shard_map(
        shards,
        mesh=mesh,
        in_specs=placed,
        out_specs=(
            P(("fsdp", "tp"), None),
            P(("fsdp", "tp"), None),
            P(("fsdp", "tp")),
            P("fsdp", "tp"),
            P("fsdp", "tp"),
            P(("fsdp", "tp"), None),
            P("fsdp", "tp"),
            P("tp", None),
            P("tp"),
            P(("fsdp", "tp"), None),
            P(("fsdp", "tp")),
            P("tp"),
            P("tp"),
            P("tp"),
            P("tp"),
            P("tp", "fsdp"),
            P("fsdp", "tp"),
            P(("fsdp", "tp"), None),
            P("tp", "fsdp"),
            P(("fsdp", "tp")),
            P("fsdp", "tp"),
            P("fsdp", "tp"),
            P("tp", "fsdp"),
        ),
        check_vma=False,
    )
```

profile of v0, /device:TPU:0, one launch (start us, length us, event | category | flops | bytes accessed | tf_op | source)
XLA Modules:
  0.0 290.5 jit_solution(6679110990700410340)
XLA Ops:
  41.1 3.7 %collective-permute-done.13.refs_1_.refs_13_ = bf16[128,1024]{1,0:T(8,128)(2,1)S(1)} collective-permute-done((bf16[128,1024]{1,0:T(8,128)(2,1)S(1)}, bf16[128,1024]{1,0:T(8,128)(2,1)S(1)}, u32[]{:S(2)}, u32[]{:S(2)}) %collective-permute-start.13) | collective-permute-done | bytes 262176 | tf_op jit(solution)/shard_map/ppermute | solution.py:49
  51.8 3.1 %collective-permute-done.15.refs_1_.refs_12_ = bf16[128,1024]{1,0:T(8,128)(2,1)} collective-permute-done((bf16[128,1024]{1,0:T(8,128)(2,1)}, bf16[128,1024]{1,0:T(8,128)(2,1)}, u32[]{:S(2)}, u32[]{:S(2)}) %collective-permute-start.15) | collective-permute-done | bytes 262176 | tf_op jit(solution)/shard_map/ppermute | solution.py:49
  58.8 4.3 %shard_map.415 = (bf16[4,256,1024]{2,1,0:T(8,128)(2,1)S(1)}, f32[4,256,896]{2,1,0:T(8,128)S(1)}, bf16[1024,896]{1,0:T(8,128)(2,1)S(1)}, f32[8,1024]{1,0:T(8,128)S(1)}, f32[8,256]{1,0:T(8,128)S(1)}) custom-call(s32[8]{0:T(128)S(1)} %fusion.11.refs_0_, bf16[256,1024]{1,0:T(8,128)(2,1)S(1)} %shard_map.409.refs_1_, ...), custom_call_target="tpu_custom_call" | custom-call | flops 6000000000 | tf_op jit(solution)/shard_map/pallas_call | solution.py:1237
  68.8 3.7 %collective-permute-done.18.refs_2_.refs_16_ = bf16[128,1024]{1,0:T(8,128)(2,1)S(1)} collective-permute-done((bf16[128,1024]{1,0:T(8,128)(2,1)S(1)}, bf16[128,1024]{1,0:T(8,128)(2,1)S(1)}, u32[]{:S(2)}, u32[]{:S(2)}) %collective-permute-start.18) | collective-permute-done | bytes 262176 | tf_op jit(solution)/shard_map/ppermute | solution.py:45
  72.5 10.8 %shard_map.421 = (f32[1024,384]{1,0:T(8,128)S(1)}, bf16[1024,384]{1,0:T(8,128)(2,1)S(1)}, bf16[1024,640]{1,0:T(8,128)(2,1)S(1)}, bf16[1024,640]{1,0:T(8,128)(2,1...) custom-call(s32[1]{0:T(128)} %bitcast.refs_0_, ...), custom_call_target="tpu_custom_call" | custom-call | flops 11000000512 | tf_op jit(solution)/shard_map/pallas_call | solution.py:1237
  83.4 13.0 %collective-permute-start.23 = (bf16[128,1536]{1,0:T(8,128)(2,1)S(1)}, bf16[128,1536]{1,0:T(8,128)(2,1)S(1)}, u32[]{:S(2)}, u32[]{:S(2)}) collective-permute-start(bf16[128,1536]{1,0:T(8,128)(2,1)S(1)} %shard_map.423.refs_18_), channel_id=1, source_target_pairs={{0,8},{4,12},{8,16},{12,20},{16,24},{20,28},{24,0},{28,4},{1,9},{5... | collective-permute-start | bytes 1179656 | tf_op jit(solution)/shard_map/ppermute | solution.py:49
  97.6 8.4 %shard_map.425 = (bf16[4,256,512]{2,1,0:T(8,128)(2,1)S(1)}, bf16[4,256,384]{2,1,0:T(8,128)(2,1)S(1)}, bf16[1024,384]{1,0:T(8,128)(2,1)S(1)}, bf16[1024,128]{1,0:...) custom-call(s32[1]{0:T(128)} %bitcast.refs_0_, ...), custom_call_target="tpu_custom_call" | custom-call | flops 8999999488 | tf_op jit(solution)/shard_map/pallas_call | solution.py:1237
  111.8 2.7 collective-permute-start.27
  115.5 9.2 %collective-permute-done.27.refs_1_.refs_6_ = bf16[128,1536]{1,0:T(8,128)(2,1)S(1)} collective-permute-done((bf16[128,1536]{1,0:T(8,128)(2,1)S(1)}, bf16[128,1536]{1,0:T(8,128)(2,1)S(1)}, u32[]{:S(2)}, u32[]{:S(2)}) %collective-permute-start.27) | collective-permute-done | bytes 393248 | tf_op jit(solution)/shard_map/ppermute | solution.py:49
  127.9 9.9 %collective-permute-done.32.refs_10_ = bf16[128,1536]{1,0:T(8,128)(2,1)S(1)} collective-permute-done((bf16[128,1536]{1,0:T(8,128)(2,1)S(1)}, bf16[128,1536]{1,0:T(8,128)(2,1)S(1)}, u32[]{:S(2)}, u32[]{:S(2)}) %collective-permute-start.32) | collective-permute-done | bytes 393248 | tf_op jit(solution)/shard_map/ppermute | solution.py:45
  137.8 3.5 %shard_map.431 = (bf16[4,256,1024]{2,1,0:T(8,128)(2,1)S(1)}, bf16[4,256,1024]{2,1,0:T(8,128)(2,1)S(1)}, bf16[4,256,512]{2,1,0:T(8,128)(2,1)S(1)}, bf16[4,256,102...) custom-call(s32[1]{0:T(128)} %constant.85.clone.1.refs_0_, ...), custom_call_target="tpu_custom_call" | custom-call | flops 5000000000 | tf_op jit(solution)/shard_map/pallas_call | solution.py:1237
  143.3 3.4 %shard_map.433 = (bf16[4,256,1024]{2,1,0:T(8,128)(2,1)S(1)}, bf16[4,256,1024]{2,1,0:T(8,128)(2,1)S(1)}, bf16[4,256,512]{2,1,0:T(8,128)(2,1)S(1)}, bf16[4,256,102...) custom-call(s32[1]{0:T(128)} %constant.85.clone.1.refs_0_, ...), custom_call_target="tpu_custom_call", output_to_operand_aliasing={{0}: (6, {}), {1}: (7, {}), {2}: (8, {}), {3}: (9, {})} | custom-call | flops 5000000000 | tf_op jit(solution)/shard_map/pallas_call | solution.py:1237
  153.0 10.1 %collective-permute-done.38.refs_7_.refs_1_ = bf16[128,1536]{1,0:T(8,128)(2,1)S(1)} collective-permute-done((bf16[128,1536]{1,0:T(8,128)(2,1)S(1)}, bf16[128,1536]{1,0:T(8,128)(2,1)S(1)}, u32[]{:S(2)}, u32[]{:S(2)}) %collective-permute-start.38) | collective-permute-done | bytes 393248 | tf_op jit(solution)/shard_map/ppermute | solution.py:45
  167.4 2.7 collective-permute-start.42
  170.1 6.5 %collective-permute-done.41.refs_2_.refs_1_ = bf16[128,1536]{1,0:T(8,128)(2,1)S(1)} collective-permute-done((bf16[128,1536]{1,0:T(8,128)(2,1)S(1)}, bf16[128,1536]{1,0:T(8,128)(2,1)S(1)}, u32[]{:S(2)}, u32[]{:S(2)}) %collective-permute-start.41) | collective-permute-done | bytes 393248 | tf_op jit(solution)/shard_map/ppermute | solution.py:45
  176.6 2.8 collective-permute-done.42.refs_3_.refs_2_
  189.6 6.9 %shard_map.441.refs_5_.refs_2_ = bf16[4,256,256]{2,1,0:T(8,128)(2,1)S(1)} custom-call(s32[1]{0:T(128)} %bitcast.refs_0_, bf16[1024,128]{1,0:T(8,128)(2,1)S(1)} %get-tuple-element.168.refs_1_, s32[1024,1]{1,0:T(8,128)S(1)} %copy-done.9, s32[1,1024]{1,0:T(1,128)S(1)} %bitcast.73, f32[1024,128]{1,0:T(8,128)S(1)} %copy-done.7, f32[1024,128]{1,0:T(8,128)S(1)} %copy-done.1, ...), custom_call_target="tpu_custom_call" | custom-call | flops 7000000000 | tf_op jit(solution)/shard_map/pallas_call | solution.py:1237
  203.0 11.2 %shard_map.444 = (f32[384,1024]{1,0:T(8,128)S(1)}, f32[128,1024]{1,0:T(8,128)S(1)}, f32[1024,128]{1,0:T(8,128)S(1)}, f32[8,1024]{1,0:T(8,128)S(1)}, f32[384,1024]{1,0:T(8,128)S(1)}, /*index=5*/f32[8,384]{1,0:T(8,128)S(1)}) custom-call(s32[1]{0:T(128)} %bitcast.refs_0_, f32[1024,384]{1,0:T(8,128)S(1)} %get-tuple-element.173.refs_1_.refs_2_, ...), custom_call_target="tpu_custom_call" | custom-call | flops 12000000000 | tf_op jit(solution)/shard_map/pallas_call | solution.py:1237
  217.8 6.4 %shard_map.446 = (bf16[4,256,768]{2,1,0:T(8,128)(2,1)S(1)}, f32[8,384]{1,0:T(8,128)S(1)}, f32[8,256]{1,0:T(8,128)S(1)}, f32[8,128]{1,0:T(8,128)S(1)}) custom-call(s32[1]{0:T(128)} %bitcast.refs_0_, bf16[1024,640]{1,0:T(8,128)(2,1)S(1)} %get-tuple-element.172.refs_1_, f32[1024,384]{1,0:T(8,128)S(1)} %get-tuple-element.173.refs_1_.refs_2_, ...), custom_call_target="tpu_custom_call" | custom-call | flops 7000000000 | tf_op jit(solution)/shard_map/pallas_call | solution.py:1237
  227.6 5.1 %collective-permute-done.51.refs_6_.refs_2_ = bf16[144,768]{1,0:T(8,128)(2,1)S(1)} collective-permute-done((bf16[144,768]{1,0:T(8,128)(2,1)S(1)}, bf16[144,768]{1,0:T(8,128)(2,1)S(1)}, u32[]{:S(2)}, u32[]{:S(2)}) %collective-permute-start.51) | collective-permute-done | bytes 221216 | tf_op jit(solution)/shard_map/ppermute | solution.py:45
  232.7 4.5 %shard_map.449 = (f32[512,1024]{1,0:T(8,128)S(1)}, bf16[512,1024]{1,0:T(8,128)(2,1)S(1)}, f32[8,128]{1,0:T(8,128)S(1)}) custom-call(s32[1]{0:T(128)} %constant.85.clone.1.refs_0_, bf16[4,256,384]{2,1,0:T(8,128)(2,1)S(1)} %get-tuple-element.167.refs_1_, bf16[4,256,256]{2,1,0:T(8,128)(2,1)S(1)} %shard_map.441.refs_5_.refs_2_, ...), custom_call_target="tpu_custom_call" | custom-call | flops 4000000000 | tf_op jit(solution)/shard_map/pallas_call | solution.py:1237
  243.2 2.7 shard_map.456
  269.9 2.8 shard_map.454.refs_7_
  272.7 2.7 shard_map.459
  (413 shorter events, 148.1 us)
Async XLA Ops:
  17.0 24.1 %collective-permute-start.3 = (bf16[256,1024]{1,0:T(8,128)(2,1)S(1)}, bf16[256,1024]{1,0:T(8,128)(2,1)S(1)}, u32[]{:S(2)}, u32[]{:S(2)}) collective-permute-start(bf16[256,1024]{1,0:T(8,128)(2,1)S(1)} %shard_map.409.refs_1_), channel_id=1, source_target_pairs={{0,2},{1,3},{2,0},{3,1},{4,6},{5,7},{6,4},{7,5},{8,10},{9,11},{10,... | collective-permute-start | bytes 1572872 | tf_op jit(solution)/shard_map/ppermute | solution.py:45
  17.2 16.4 %collective-permute-start.4 = (bf16[256,1024]{1,0:T(8,128)(2,1)S(1)}, bf16[256,1024]{1,0:T(8,128)(2,1)}, u32[]{:S(2)}, u32[]{:S(2)}) collective-permute-start(bf16[256,1024]{1,0:T(8,128)(2,1)S(1)} %shard_map.409.refs_1_), channel_id=1, source_target_pairs={{0,1},{1,0},{2,3},{3,2},{4,5},{5,4},{6,7},{7,6},{8,9},{9,8},{10,11... | collective-permute-start | bytes 1572872 | tf_op jit(solution)/shard_map/ppermute | solution.py:45
  41.1 17.6 %collective-permute-start.5 = (bf16[256,1024]{1,0:T(8,128)(2,1)S(1)}, bf16[256,1024]{1,0:T(8,128)(2,1)}, u32[]{:S(2)}, u32[]{:S(2)}) collective-permute-start(bf16[256,1024]{1,0:T(8,128)(2,1)S(1)} %collective-permute-done.3.refs_2_), channel_id=1, source_target_pairs={{0,1},{1,0},{2,3},{3,2},{4,5},{5,4},{6,7},{7,6},{8,9},{9,8},{10,11... | collective-permute-start | bytes 1572872 | tf_op jit(solution)/shard_map/ppermute | solution.py:45
  63.7 33.8 %collective-permute-start.22 = (bf16[256,1024]{1,0:T(8,128)(2,1)S(1)}, bf16[256,1024]{1,0:T(8,128)(2,1)S(1)}, u32[]{:S(2)}, u32[]{:S(2)}) collective-permute-start(bf16[256,1024]{1,0:T(8,128)(2,1)S(1)} %shard_map.424.refs_3_), channel_id=1, source_target_pairs={{0,2},{1,3},{2,0},{3,1},{4,6},{5,7},{6,4},{7,5},{8,10},{9,11},{10,... | collective-permute-start | bytes 1572872 | tf_op jit(solution)/shard_map/ppermute | solution.py:45
  66.5 16.9 %collective-permute-start.20 = (bf16[128,1536]{1,0:T(8,128)(2,1)S(1)}, bf16[128,1536]{1,0:T(8,128)(2,1)S(1)}, u32[]{:S(2)}, u32[]{:S(2)}) collective-permute-start(bf16[128,1536]{1,0:T(8,128)(2,1)S(1)} %shard_map.422), channel_id=1, source_target_pairs={{0,8},{4,12},{8,16},{12,20},{16,24},{20,28},{24,0},{28,4},{1,9},{5... | collective-permute-start | bytes 1179656 | tf_op jit(solution)/shard_map/ppermute | solution.py:49
  67.7 15.7 %collective-permute-start.21 = (bf16[128,1536]{1,0:T(8,128)(2,1)S(1)}, bf16[128,1536]{1,0:T(8,128)(2,1)S(1)}, u32[]{:S(2)}, u32[]{:S(2)}) collective-permute-start(bf16[128,1536]{1,0:T(8,128)(2,1)S(1)} %shard_map.422), channel_id=1, source_target_pairs={{0,4},{4,0},{8,12},{12,8},{16,20},{20,16},{24,28},{28,24},{1,5},{5... | collective-permute-start | bytes 1179656 | tf_op jit(solution)/shard_map/ppermute | solution.py:45
  83.4 22.6 %collective-permute-start.23 = (bf16[128,1536]{1,0:T(8,128)(2,1)S(1)}, bf16[128,1536]{1,0:T(8,128)(2,1)S(1)}, u32[]{:S(2)}, u32[]{:S(2)}) collective-permute-start(bf16[128,1536]{1,0:T(8,128)(2,1)S(1)} %shard_map.423.refs_18_), channel_id=1, source_target_pairs={{0,8},{4,12},{8,16},{12,20},{16,24},{20,28},{24,0},{28,4},{1,9},{5... | collective-permute-start | bytes 1179656 | tf_op jit(solution)/shard_map/ppermute | solution.py:49
  110.2 14.9 %collective-permute-start.26 = (bf16[256,1024]{1,0:T(8,128)(2,1)S(1)}, bf16[256,1024]{1,0:T(8,128)(2,1)S(1)}, u32[]{:S(2)}, u32[]{:S(2)}) collective-permute-start(bf16[256,1024]{1,0:T(8,128)(2,1)S(1)} %shard_map.428), channel_id=1, source_target_pairs={{0,2},{1,3},{2,0},{3,1},{4,6},{5,7},{6,4},{7,5},{8,10},{9,11},{10,... | collective-permute-start | bytes 1572872 | tf_op jit(solution)/shard_map/ppermute | solution.py:45
  111.8 12.9 %collective-permute-start.27 = (bf16[128,1536]{1,0:T(8,128)(2,1)S(1)}, bf16[128,1536]{1,0:T(8,128)(2,1)S(1)}, u32[]{:S(2)}, u32[]{:S(2)}) collective-permute-start(bf16[128,1536]{1,0:T(8,128)(2,1)S(1)} %shard_map.427.refs_2_), channel_id=1, source_target_pairs={{0,8},{4,12},{8,16},{12,20},{16,24},{20,28},{24,0},{28,4},{1,9},{5... | collective-permute-start | bytes 1179656 | tf_op jit(solution)/shard_map/ppermute | solution.py:49
  114.9 13.0 %collective-permute-start.31 = (bf16[256,1024]{1,0:T(8,128)(2,1)S(1)}, bf16[256,1024]{1,0:T(8,128)(2,1)S(1)}, u32[]{:S(2)}, u32[]{:S(2)}) collective-permute-start(bf16[256,1024]{1,0:T(8,128)(2,1)S(1)} %shard_map.424.refs_3_), channel_id=1, source_target_pairs={{0,1},{1,0},{2,3},{3,2},{4,5},{5,4},{6,7},{7,6},{8,9},{9,8},{10,11... | collective-permute-start | bytes 1572872 | tf_op jit(solution)/shard_map/ppermute | solution.py:45
  126.7 14.6 %collective-permute-start.29 = (bf16[256,1024]{1,0:T(8,128)(2,1)S(1)}, bf16[256,1024]{1,0:T(8,128)(2,1)S(1)}, u32[]{:S(2)}, u32[]{:S(2)}) collective-permute-start(bf16[256,1024]{1,0:T(8,128)(2,1)S(1)} %get-tuple-element.144.refs_1_), channel_id=1, source_target_pairs={{0,2},{1,3},{2,0},{3,1},{4,6},{5,7},{6,4},{7,5},{8,10},{9,11},{10,... | collective-permute-start | bytes 1572872 | tf_op jit(solution)/shard_map/ppermute | solution.py:45
  127.9 14.0 %collective-permute-start.34 = (bf16[256,1024]{1,0:T(8,128)(2,1)S(1)}, bf16[256,1024]{1,0:T(8,128)(2,1)S(1)}, u32[]{:S(2)}, u32[]{:S(2)}) collective-permute-start(bf16[256,1024]{1,0:T(8,128)(2,1)S(1)} %collective-permute-done.22.refs_19_.refs_3_), channel_id=1, source_target_pairs={{0,1},{1,0},{2,3},{3,2},{4,5},{5,4},{6,7},{7,6},{8,9},{9,8},{10,11... | collective-permute-start | bytes 1572872 | tf_op jit(solution)/shard_map/ppermute | solution.py:45
  149.6 14.3 %collective-permute-start.37 = (bf16[256,1024]{1,0:T(8,128)(2,1)S(1)}, bf16[256,1024]{1,0:T(8,128)(2,1)S(1)}, u32[]{:S(2)}, u32[]{:S(2)}) collective-permute-start(bf16[256,1024]{1,0:T(8,128)(2,1)S(1)} %add_convert_fusion.2), channel_id=1, source_target_pairs={{0,2},{1,3},{2,0},{3,1},{4,6},{5,7},{6,4},{7,5},{8,10},{9,11},{10,... | collective-permute-start | bytes 1572872 | tf_op jit(solution)/shard_map/ppermute | solution.py:45
  165.1 14.4 %collective-permute-start.39 = (bf16[256,1024]{1,0:T(8,128)(2,1)S(1)}, bf16[256,1024]{1,0:T(8,128)(2,1)S(1)}, u32[]{:S(2)}, u32[]{:S(2)}) collective-permute-start(bf16[256,1024]{1,0:T(8,128)(2,1)S(1)} %get-tuple-element.159.refs_2_), channel_id=1, source_target_pairs={{0,2},{1,3},{2,0},{3,1},{4,6},{5,7},{6,4},{7,5},{8,10},{9,11},{10,... | collective-permute-start | bytes 1572872 | tf_op jit(solution)/shard_map/ppermute | solution.py:45
  180.2 18.6 %collective-permute-start.46 = (bf16[128,1536]{1,0:T(8,128)(2,1)S(1)}, bf16[128,1536]{1,0:T(8,128)(2,1)S(1)}, u32[]{:S(2)}, u32[]{:S(2)}) collective-permute-start(bf16[128,1536]{1,0:T(8,128)(2,1)S(1)} %get-tuple-element.178), channel_id=1, source_target_pairs={{0,4},{4,0},{8,12},{12,8},{16,20},{20,16},{24,28},{28,24},{1,5},{5... | collective-permute-start | bytes 1179656 | tf_op jit(solution)/shard_map/ppermute | solution.py:45
  181.2 17.5 %collective-permute-start.47 = (bf16[128,1536]{1,0:T(8,128)(2,1)S(1)}, bf16[128,1536]{1,0:T(8,128)(2,1)S(1)}, u32[]{:S(2)}, u32[]{:S(2)}) collective-permute-start(bf16[128,1536]{1,0:T(8,128)(2,1)S(1)} %get-tuple-element.163.refs_9_), channel_id=1, source_target_pairs={{0,8},{4,12},{8,16},{12,20},{16,24},{20,28},{24,0},{28,4},{1,9},{5... | collective-permute-start | bytes 1179656 | tf_op jit(solution)/shard_map/ppermute | solution.py:49
  186.6 14.5 %collective-permute-start.44 = (bf16[512,1024]{1,0:T(8,128)(2,1)S(1)}, bf16[512,1024]{1,0:T(8,128)(2,1)S(1)}, u32[]{:S(2)}, u32[]{:S(2)}) collective-permute-start(bf16[512,1024]{1,0:T(8,128)(2,1)S(1)} %get-tuple-element.166), channel_id=1, source_target_pairs={{0,1},{1,0},{2,3},{3,2},{4,5},{5,4},{6,7},{7,6},{8,9},{9,8},{10,11... | collective-permute-start | bytes 3145736 | tf_op jit(solution)/shard_map/ppermute | solution.py:45
  197.7 16.6 %collective-permute-start.48 = (bf16[128,1152]{1,0:T(8,128)(2,1)S(1)}, bf16[128,1152]{1,0:T(8,128)(2,1)S(1)}, u32[]{:S(2)}, u32[]{:S(2)}) collective-permute-start(bf16[128,1152]{1,0:T(8,128)(2,1)S(1)} %shard_map.443.refs_11_), channel_id=1, source_target_pairs={{0,4},{4,0},{8,12},{12,8},{16,20},{20,16},{24,28},{28,24},{1,5},{5... | collective-permute-start | bytes 884744 | tf_op jit(solution)/shard_map/ppermute | solution.py:45
  199.3 18.5 %collective-permute-start.49 = (bf16[128,1536]{1,0:T(8,128)(2,1)S(1)}, bf16[128,1536]{1,0:T(8,128)(2,1)S(1)}, u32[]{:S(2)}, u32[]{:S(2)}) collective-permute-start(bf16[128,1536]{1,0:T(8,128)(2,1)S(1)} %get-tuple-element.188), channel_id=1, source_target_pairs={{0,4},{4,0},{8,12},{12,8},{16,20},{20,16},{24,28},{28,24},{1,5},{5... | collective-permute-start | bytes 1179656 | tf_op jit(solution)/shard_map/ppermute | solution.py:45
  200.4 17.4 %collective-permute-start.50 = (bf16[128,1536]{1,0:T(8,128)(2,1)S(1)}, bf16[128,1536]{1,0:T(8,128)(2,1)S(1)}, u32[]{:S(2)}, u32[]{:S(2)}) collective-permute-start(bf16[128,1536]{1,0:T(8,128)(2,1)S(1)} %get-tuple-element.179.refs_10_), channel_id=1, source_target_pairs={{0,8},{4,12},{8,16},{12,20},{16,24},{20,28},{24,0},{28,4},{1,9},{5... | collective-permute-start | bytes 1179656 | tf_op jit(solution)/shard_map/ppermute | solution.py:49
  201.2 16.6 %collective-permute-start.45 = (bf16[256,1024]{1,0:T(8,128)(2,1)S(1)}, bf16[256,1024]{1,0:T(8,128)(2,1)S(1)}, u32[]{:S(2)}, u32[]{:S(2)}) collective-permute-start(bf16[256,1024]{1,0:T(8,128)(2,1)S(1)} %add_convert_fusion.1.refs_12_), channel_id=1, source_target_pairs={{0,2},{1,3},{2,0},{3,1},{4,6},{5,7},{6,4},{7,5},{8,10},{9,11},{10,... | collective-permute-start | bytes 1572872 | tf_op jit(solution)/shard_map/ppermute | solution.py:45
  242.4 22.8 %collective-permute-start.55 = (bf16[256,1024]{1,0:T(8,128)(2,1)}, bf16[256,1024]{1,0:T(8,128)(2,1)}, u32[]{:S(2)}, u32[]{:S(2)}) collective-permute-start(bf16[256,1024]{1,0:T(8,128)(2,1)} %add_convert_fusion.refs_5_.refs_6_), channel_id=1, source_target_pairs={{0,2},{1,3},{2,0},{3,1},{4,6},{5,7},{6,4},{7,5},{8,10},{9,11},{10,... | collective-permute-start | bytes 1572872 | tf_op jit(solution)/shard_map/ppermute | solution.py:45
  246.0 14.3 %collective-permute-start.62 = (bf16[128,1152]{1,0:T(8,128)(2,1)}, bf16[128,1152]{1,0:T(8,128)(2,1)}, u32[]{:S(2)}, u32[]{:S(2)}) collective-permute-start(bf16[128,1152]{1,0:T(8,128)(2,1)} %get-tuple-element.210), channel_id=1, source_target_pairs={{0,4},{4,0},{8,12},{12,8},{16,20},{20,16},{24,28},{28,24},{1,5},{5... | collective-permute-start | bytes 884744 | tf_op jit(solution)/shard_map/ppermute | solution.py:45
  247.1 13.2 %collective-permute-start.63 = (bf16[128,1152]{1,0:T(8,128)(2,1)}, bf16[128,1152]{1,0:T(8,128)(2,1)}, u32[]{:S(2)}, u32[]{:S(2)}) collective-permute-start(bf16[128,1152]{1,0:T(8,128)(2,1)} %get-tuple-element.211), channel_id=1, source_target_pairs={{0,8},{4,12},{8,16},{12,20},{16,24},{20,28},{24,0},{28,4},{1,9},{5... | collective-permute-start | bytes 884744 | tf_op jit(solution)/shard_map/ppermute | solution.py:49
  (131 other events, 1535.1 us)
where the time goes:
time: 294 us; the launch traced here: 290 us
  Pallas kernels  102 us (35%)
  starting transfers between devices  73.1 us (25%)
  waiting for transfers between devices  70.9 us (24%)
  local copies, waits for them, and re-layouts  21.7 us (7%)
  other arithmetic  11.9 us (4%)
  matrix products  8.97 us (3%)
    pallas_call x55, Pallas kernels, call_kernel(): pl.pallas_call(wrapped, out_shape=shapes, in_specs=[pl.BlockSpec(memory_s...  102 us
    ppermute x50, waiting for transfers between devices, flip(): return lax.ppermute(values, axis, [(i, i ^ mask) for i in range(size)])  47.1 us
    ppermute x50, starting transfers between devices, flip(): return lax.ppermute(values, axis, [(i, i ^ mask) for i in range(size)])  38.1 us
    ppermute x18, starting transfers between devices, ring(): lax.ppermute(values, 'fsdp', [(i, (i + 2 * step) % 8) for i in range(8)])  35 us
    ppermute x18, waiting for transfers between devices, ring(): lax.ppermute(values, 'fsdp', [(i, (i + 2 * step) % 8) for i in range(8)])  23.8 us
    unnamed x177, local copies, waits for them, and re-layouts  10.1 us
    dot_general x6, matrix products, contract_rows(): lax.dot_general(left_side, right_side, (((0,), (0,)), ((), ())), preferre...  8.97 us
  transfers between devices with their start and end apart: 68, of which 23 were waited for; matrix products, arithmetic and copies ran while one was open for 9% of the time, Pallas kernels for 31%

commit v1 on v0

--- a/solution.py
+++ b/solution.py
@@ -685,14 +685,14 @@
     for i in range(blocks):
         width = (i + 1) * size
         rows = slice(i * size, width)
-        query = query_ref[rows]
+        query = query_ref[rows] * HEAD ** (-0.5)
         places = row_ids(size, width) + i * size
         allowed = (segc_ref[rows] == segr_ref[:, :width]) & (places >= lane_ids(size, width))
         outs, logs = [], []
         for h in range(2):
             mine = (lanes < HEAD) if h == 0 else (lanes >= HEAD)
             masked = jnp.where(mine, query, jnp.zeros_like(query))
-            scores = dot_nt(masked, keyk_ref[:width]) * HEAD ** (-0.5)
+            scores = dot_nt(masked, keyk_ref[:width])
             scores = jnp.where(allowed, scores, NEG_FILL)
             top = jnp.max(scores, axis=-1, keepdims=True)
             powers = jnp.exp(scores - top)
@@ -777,7 +777,7 @@
     for i in range(blocks):
         width = (i + 1) * size
         rows = slice(i * size, width)
-        query = query_ref[rows]
+        query = query_ref[rows] * HEAD ** (-0.5)
         d_att = datt_ref[rows]
         logs = logs_ref[rows]
         places = row_ids(size, width) + i * size
@@ -787,7 +787,7 @@
             mine = (lanes < HEAD) if h == 0 else (lanes >= HEAD)
             masked = jnp.where(mine, query, jnp.zeros_like(query))
             d_masked = jnp.where(mine, d_att, jnp.zeros_like(d_att))
-            scores = dot_nt(masked, keyk_ref[:width]) * HEAD ** (-0.5)
+            scores = dot_nt(masked, keyk_ref[:width])
             scores = jnp.where(allowed, scores, NEG_FILL)
             probs = jnp.exp(scores - logs[:, h * HEAD : h * HEAD + 1])
             d_probs = dot_nt(d_masked, valv_ref[:width])
@@ -804,7 +804,7 @@
     def key_block(a, carry):
         rows = pl.ds(pl.multiple_of(a * size, size), size)
         d_key, d_val = dkey[rows], dval[rows]
-        d_key = (d_key + pltpu.roll(d_key, HEAD, 1)) * HEAD ** (-0.5)
+        d_key = d_key + pltpu.roll(d_key, HEAD, 1)
         d_val = d_val + pltpu.roll(d_val, HEAD, 1)
         d_key = d_key * cos_ref[rows] - swap_halves(d_key, lanes) * sin_ref[rows]
         dproj_ref[piece_at(a, at), :, 128:] = jnp.where(lanes < HEAD, d_key, d_val).astype(
@@ -1061,18 +1061,22 @@
     for p, piece in enumerate(pieces):
         first = (piece[...].astype(jnp.float32) * gain).astype(jnp.bfloat16)
         first_ref[p] = first
-        proj_ref[p] = dot_nn(first, weight_ref[...])
-    feature = row_ids(width, states)
+    whole = first_ref[...].reshape(4 * rows, width)
+    proj_ref[...] = dot_nn(whole, weight_ref[...]).reshape(proj_ref.shape)
     block = width // 8
-    place = feature % block
-    for b in range(8):
-        place = place + jnp.where(feature // block == b, order_ref[b] * block, 0)
-    channel = lane_ids(width, states)
+    aim = lane_ids(block, states) * CONV - row_ids(block, states)
+    bits = small.astype(jnp.bfloat16)
     taps = []
-    for k in range(CONV + 1):
-        picked = jnp.where(place == channel * CONV + k % CONV, 1.0, 0.0).astype(jnp.bfloat16)
-        found = dot_nn(small.astype(jnp.bfloat16), picked)
-        taps.append(found[2:3] if k < CONV else found[3:4])
+    for k in range(CONV):
+        picked = [
+            jnp.where(aim == order_ref[b] * block - k, 1.0, 0.0).astype(jnp.bfloat16)
+            for b in range(8)
+        ]
+        found = dot_nn(bits, jnp.concatenate(picked, axis=0))
+        taps.append(found[2:3])
+        if k == 0:
+            offset = found[3:4]
+    taps.append(offset)
     taps.append(jnp.zeros((8 - len(taps), states), jnp.float32))
     taps_ref[...] = jnp.concatenate(taps, axis=0)
 
@@ -1094,16 +1098,18 @@
     token_ref[...] = jnp.zeros_like(token_ref)
     rows, channels = gate_ref.shape[1], gate_ref.shape[2]
     wide = channels + 128
-    for p in (3, 2, 1, 0):
-        result = dot_nt(gate_ref[p], late_ref[:, :channels])
-        result = result + dot_nt(attn_ref[p, :, :128], late_ref[:, channels:wide])
-        result = result + dot_nt(attn_ref[p, :, 128:], weight_ref[:, channels:wide])
-        result = result + dot_nt(scan_ref[p, :, :channels], weight_ref[:, :channels])
-        result = result + dot_nt(scan_ref[p, :, channels:], weight_ref[:, wide:])
-        if p < 2:
-            keep_ref[p * rows : p * rows + rows] = result
-        else:
-            give_ref[p * rows - 2 * rows : p * rows - rows] = result.astype(jnp.bfloat16)
+
+    def pair(ref, at):
+        return ref[at : at + 2].reshape(2 * rows, ref.shape[2])
+
+    for at, out_ref in ((2, give_ref), (0, keep_ref)):
+        attn, scan = pair(attn_ref, at), pair(scan_ref, at)
+        result = dot_nt(pair(gate_ref, at), late_ref[:, :channels])
+        result = result + dot_nt(attn[:, :128], late_ref[:, channels:wide])
+        result = result + dot_nt(attn[:, 128:], weight_ref[:, channels:wide])
+        result = result + dot_nt(scan[:, :channels], weight_ref[:, :channels])
+        result = result + dot_nt(scan[:, channels:], weight_ref[:, wide:])
+        out_ref[...] = result.astype(out_ref.dtype)
 
 
 def ffn_body(slots, fresh, _, *refs):
@@ -1119,26 +1125,28 @@
     rows = second_ref.shape[1]
     gate_up_weight = weight_ref.at[:, : 2 * hidden_local]
     down_weight = weight_ref.at[:, 2 * hidden_local :]
-    for p, piece, cots_ref in zip(slots, pieces, cots):
-        values, cot = piece[...], cots_ref[...]
-        second_ref[p] = values
-        cot_ref[p] = cot
-        gate_up = dot_nn(values, gate_up_weight[...])
-        d_hidden = dot_nn(cot, down_weight[...])
-        gate, up = gate_up[:, :hidden_local], gate_up[:, hidden_local:]
-        sig = jax.nn.sigmoid(gate)
-        act = gate * sig
-        hidden = (act * up).astype(jnp.bfloat16)
-        hidden_ref[p] = hidden
-        d_gate = (d_hidden * up * sig * (1.0 + gate * (1.0 - sig))).astype(jnp.bfloat16)
-        d_up = (d_hidden * act).astype(jnp.bfloat16)
-        dgu_ref[p, :, :hidden_local] = d_gate
-        dgu_ref[p, :, hidden_local:] = d_up
-        d_second = dot_nt(dgu_ref[p], gate_up_weight[...])
+    values = jnp.concatenate([piece[...] for piece in pieces], axis=0)
+    cot = jnp.concatenate([cots_ref[...] for cots_ref in cots], axis=0)
+    gate_up = dot_nn(values, gate_up_weight[...])
+    d_hidden = dot_nn(cot, down_weight[...])
+    gate, up = gate_up[:, :hidden_local], gate_up[:, hidden_local:]
+    sig = jax.nn.sigmoid(gate)
+    act = gate * sig
+    hidden = (act * up).astype(jnp.bfloat16)
+    d_gate = (d_hidden * up * sig * (1.0 + gate * (1.0 - sig))).astype(jnp.bfloat16)
+    d_up = (d_hidden * act).astype(jnp.bfloat16)
+    d_gate_up = jnp.concatenate([d_gate, d_up], axis=1)
+    d_second = dot_nt(d_gate_up, gate_up_weight[...])
+    for k, p in enumerate(slots):
+        here = slice(k * rows, k * rows + rows)
+        second_ref[p] = values[here]
+        cot_ref[p] = cot[here]
+        hidden_ref[p] = hidden[here]
+        dgu_ref[p] = d_gate_up[here]
         if p < 2:
-            dkeep[...] = d_second
+            dkeep[...] = d_second[here]
         else:
-            dgive[...] = d_second.astype(jnp.bfloat16)
+            dgive[...] = d_second[here].astype(jnp.bfloat16)
 
 
 def pick_rows(values, block, rows):
@@ -1323,10 +1331,6 @@
 
     row_half = ((rows, width), half_type)
     row_full = ((rows, width), full_type)
-    normed_mine, tok_rows, cot_mine = call_kernel(
-        front_body, [row_half, row_half, row_half], [], order, tokens, cotangent
-    )
-
     small = jnp.stack([norm_gain, ffn_gain, conv_bc.reshape(-1), jnp.repeat(conv_bias_bc, CONV)], 1)
     shared_in = jnp.concatenate(
         [w_keyval, w_bc, jnp.pad(small, ((0, 0), (8, 116)))], axis=1
@@ -1344,7 +1348,6 @@
             far,
             cross,
             step_wide,
-            deps=[normed_mine],
             micros=1,
         )
     else:
@@ -1362,6 +1365,10 @@
             ],
             axis=1,
         )
+    normed_mine, tok_rows, cot_mine = call_kernel(
+        front_body, [row_half, row_half, row_half], [], order, tokens, cotangent, deps=[shared_shard]
+    )
+
     def pack(turned, *shards, deps=()):
         width_all = sum(shard.size for shard in shards) // w_x.shape[0]
         return call_kernel(
@@ -1375,7 +1382,7 @@
         )[0]
 
     gather = Gather(jnp.concatenate([w_x.astype(half_type), shared_shard], axis=1))
-    normed = gather_pieces(after(normed_mine, shared_shard))
+    normed = gather_pieces(normed_mine)
     late_gather = Gather(
         pack((2, 3), w_z, w_query, w_mixer_out, w_attn_out, deps=[shared_shard, normed[2]])
     )

time: 294 us -> 292 us (level)
    unnamed x177 -> x169, local copies, waits for them, and re-layouts: 10.1 us -> 8.76 us
    pallas_call x55 -> x54, Pallas kernels: 102 us -> 101 us  [call_kernel(): pl.pallas_call(wrapped, out_shape=shapes, in_specs=[pl.BlockSpec(memory_s...]
  transfers between devices with their start and end apart: 68 -> 68, of which waited for: 23 -> 22; matrix products, arithmetic and copies ran while one was open for 9% -> 10% of each run, Pallas kernels for 31% -> 31%
where the time goes in v1:
time: 292 us; the launch traced here: 289 us
  Pallas kernels  101 us (35%)
  starting transfers between devices  73.1 us (25%)
  waiting for transfers between devices  69.5 us (24%)
  local copies, waits for them, and re-layouts  20.3 us (7%)
  other arithmetic  13.5 us (5%)
  matrix products  8.97 us (3%)
    pallas_call x54, Pallas kernels, call_kernel(): pl.pallas_call(wrapped, out_shape=shapes, in_specs=[pl.BlockSpec(memory_s...  101 us
    ppermute x50, waiting for transfers between devices, flip(): return lax.ppermute(values, axis, [(i, i ^ mask) for i in range(size)])  45.7 us
    ppermute x50, starting transfers between devices, flip(): return lax.ppermute(values, axis, [(i, i ^ mask) for i in range(size)])  39.4 us
    ppermute x18, starting transfers between devices, ring(): lax.ppermute(values, 'fsdp', [(i, (i + 2 * step) % 8) for i in range(8)])  33.7 us
    ppermute x18, waiting for transfers between devices, ring(): lax.ppermute(values, 'fsdp', [(i, (i + 2 * step) % 8) for i in range(8)])  23.8 us
    dot_general x6, matrix products, contract_rows(): lax.dot_general(left_side, right_side, (((0,), (0,)), ((), ())), preferre...  8.97 us
    unnamed x169, local copies, waits for them, and re-layouts  8.76 us
  transfers between devices with their start and end apart: 68, of which 22 were waited for; matrix products, arithmetic and copies ran while one was open for 10% of the time, Pallas kernels for 31%

profile of v1, /device:TPU:0, one launch (start us, length us, event | category | flops | bytes accessed | tf_op | source)
XLA Modules:
  0.0 288.8 jit_solution(13238448115880384827)
XLA Ops:
  40.5 3.6 %collective-permute-done.13.refs_1_.refs_13_ = bf16[128,1024]{1,0:T(8,128)(2,1)S(1)} collective-permute-done((bf16[128,1024]{1,0:T(8,128)(2,1)S(1)}, bf16[128,1024]{1,0:T(8,128)(2,1)S(1)}, u32[]{:S(2)}, u32[]{:S(2)}) %collective-permute-start.13) | collective-permute-done | bytes 262176 | tf_op jit(solution)/shard_map/ppermute | solution.py:49
  51.2 3.1 %collective-permute-done.15.refs_1_.refs_12_ = bf16[128,1024]{1,0:T(8,128)(2,1)} collective-permute-done((bf16[128,1024]{1,0:T(8,128)(2,1)}, bf16[128,1024]{1,0:T(8,128)(2,1)}, u32[]{:S(2)}, u32[]{:S(2)}) %collective-permute-start.15) | collective-permute-done | bytes 262176 | tf_op jit(solution)/shard_map/ppermute | solution.py:49
  58.2 4.1 %shard_map.414 = (bf16[4,256,1024]{2,1,0:T(8,128)(2,1)S(1)}, f32[4,256,896]{2,1,0:T(8,128)S(1)}, bf16[1024,896]{1,0:T(8,128)(2,1)S(1)}, f32[8,1024]{1,0:T(8,128)S(1)}, f32[8,256]{1,0:T(8,128)S(1)}) custom-call(s32[8]{0:T(128)S(1)} %fusion.11.refs_0_, bf16[256,1024]{1,0:T(8,128)(2,1)S(1)} %get-tuple-element.129.refs_1_, ...), custom_call_target="tpu_custom_call" | custom-call | flops 6000000000 | tf_op jit(solution)/shard_map/pallas_call | solution.py:1245
  68.0 3.6 %collective-permute-done.18.refs_2_.refs_16_ = bf16[128,1024]{1,0:T(8,128)(2,1)S(1)} collective-permute-done((bf16[128,1024]{1,0:T(8,128)(2,1)S(1)}, bf16[128,1024]{1,0:T(8,128)(2,1)S(1)}, u32[]{:S(2)}, u32[]{:S(2)}) %collective-permute-start.18) | collective-permute-done | bytes 262176 | tf_op jit(solution)/shard_map/ppermute | solution.py:45
  71.7 10.8 %shard_map.420 = (f32[1024,384]{1,0:T(8,128)S(1)}, bf16[1024,384]{1,0:T(8,128)(2,1)S(1)}, bf16[1024,640]{1,0:T(8,128)(2,1)S(1)}, bf16[1024,640]{1,0:T(8,128)(2,1...) custom-call(s32[1]{0:T(128)} %bitcast.refs_0_, ...), custom_call_target="tpu_custom_call" | custom-call | flops 11000000512 | tf_op jit(solution)/shard_map/pallas_call | solution.py:1245
  82.6 12.6 %collective-permute-start.23 = (bf16[128,1536]{1,0:T(8,128)(2,1)S(1)}, bf16[128,1536]{1,0:T(8,128)(2,1)S(1)}, u32[]{:S(2)}, u32[]{:S(2)}) collective-permute-start(bf16[128,1536]{1,0:T(8,128)(2,1)S(1)} %shard_map.422.refs_18_), channel_id=1, source_target_pairs={{0,8},{4,12},{8,16},{12,20},{16,24},{20,28},{24,0},{28,4},{1,9},{5... | collective-permute-start | bytes 1179656 | tf_op jit(solution)/shard_map/ppermute | solution.py:49
  96.3 8.4 %shard_map.424 = (bf16[4,256,512]{2,1,0:T(8,128)(2,1)S(1)}, bf16[4,256,384]{2,1,0:T(8,128)(2,1)S(1)}, bf16[1024,384]{1,0:T(8,128)(2,1)S(1)}, bf16[1024,128]{1,0:...) custom-call(s32[1]{0:T(128)} %bitcast.refs_0_, ...), custom_call_target="tpu_custom_call" | custom-call | flops 8999999488 | tf_op jit(solution)/shard_map/pallas_call | solution.py:1245
  110.4 2.7 collective-permute-start.27
  114.1 9.2 %collective-permute-done.27.refs_1_.refs_6_ = bf16[128,1536]{1,0:T(8,128)(2,1)S(1)} collective-permute-done((bf16[128,1536]{1,0:T(8,128)(2,1)S(1)}, bf16[128,1536]{1,0:T(8,128)(2,1)S(1)}, u32[]{:S(2)}, u32[]{:S(2)}) %collective-permute-start.27) | collective-permute-done | bytes 393248 | tf_op jit(solution)/shard_map/ppermute | solution.py:49
  126.6 9.8 %collective-permute-done.32.refs_10_ = bf16[128,1536]{1,0:T(8,128)(2,1)S(1)} collective-permute-done((bf16[128,1536]{1,0:T(8,128)(2,1)S(1)}, bf16[128,1536]{1,0:T(8,128)(2,1)S(1)}, u32[]{:S(2)}, u32[]{:S(2)}) %collective-permute-start.32) | collective-permute-done | bytes 393248 | tf_op jit(solution)/shard_map/ppermute | solution.py:45
  136.5 3.3 %shard_map.430 = (bf16[4,256,1024]{2,1,0:T(8,128)(2,1)S(1)}, bf16[4,256,1024]{2,1,0:T(8,128)(2,1)S(1)}, bf16[4,256,512]{2,1,0:T(8,128)(2,1)S(1)}, bf16[4,256,102...) custom-call(s32[1]{0:T(128)} %constant.88.clone.1.refs_0_, ...), custom_call_target="tpu_custom_call" | custom-call | flops 5000000000 | tf_op jit(solution)/shard_map/pallas_call | solution.py:1245
  141.8 3.3 %shard_map.432 = (bf16[4,256,1024]{2,1,0:T(8,128)(2,1)S(1)}, bf16[4,256,1024]{2,1,0:T(8,128)(2,1)S(1)}, bf16[4,256,512]{2,1,0:T(8,128)(2,1)S(1)}, bf16[4,256,102...) custom-call(s32[1]{0:T(128)} %constant.88.clone.1.refs_0_, ...), custom_call_target="tpu_custom_call", output_to_operand_aliasing={{0}: (6, {}), {1}: (7, {}), {2}: (8, {}), {3}: (9, {})} | custom-call | flops 5000000000 | tf_op jit(solution)/shard_map/pallas_call | solution.py:1245
  151.4 10.1 %collective-permute-done.38.refs_7_.refs_1_ = bf16[128,1536]{1,0:T(8,128)(2,1)S(1)} collective-permute-done((bf16[128,1536]{1,0:T(8,128)(2,1)S(1)}, bf16[128,1536]{1,0:T(8,128)(2,1)S(1)}, u32[]{:S(2)}, u32[]{:S(2)}) %collective-permute-start.38) | collective-permute-done | bytes 393248 | tf_op jit(solution)/shard_map/ppermute | solution.py:45
  165.9 2.7 collective-permute-start.42
  168.6 6.6 %collective-permute-done.41.refs_2_.refs_1_ = bf16[128,1536]{1,0:T(8,128)(2,1)S(1)} collective-permute-done((bf16[128,1536]{1,0:T(8,128)(2,1)S(1)}, bf16[128,1536]{1,0:T(8,128)(2,1)S(1)}, u32[]{:S(2)}, u32[]{:S(2)}) %collective-permute-start.41) | collective-permute-done | bytes 393248 | tf_op jit(solution)/shard_map/ppermute | solution.py:45
  175.2 2.7 collective-permute-done.42.refs_3_.refs_2_
  188.1 6.9 %shard_map.440.refs_5_.refs_2_ = bf16[4,256,256]{2,1,0:T(8,128)(2,1)S(1)} custom-call(s32[1]{0:T(128)} %bitcast.refs_0_, bf16[1024,128]{1,0:T(8,128)(2,1)S(1)} %get-tuple-element.168.refs_1_, s32[1024,1]{1,0:T(8,128)S(1)} %copy-done.9, s32[1,1024]{1,0:T(1,128)S(1)} %bitcast.73, f32[1024,128]{1,0:T(8,128)S(1)} %copy-done.7, f32[1024,128]{1,0:T(8,128)S(1)} %copy-done.1, ...), custom_call_target="tpu_custom_call" | custom-call | flops 7000000000 | tf_op jit(solution)/shard_map/pallas_call | solution.py:1245
  201.6 11.2 %shard_map.443 = (f32[384,1024]{1,0:T(8,128)S(1)}, f32[128,1024]{1,0:T(8,128)S(1)}, f32[1024,128]{1,0:T(8,128)S(1)}, f32[8,1024]{1,0:T(8,128)S(1)}, f32[384,1024]{1,0:T(8,128)S(1)}, /*index=5*/f32[8,384]{1,0:T(8,128)S(1)}) custom-call(s32[1]{0:T(128)} %bitcast.refs_0_, f32[1024,384]{1,0:T(8,128)S(1)} %get-tuple-element.173.refs_1_.refs_2_, ...), custom_call_target="tpu_custom_call" | custom-call | flops 12000000000 | tf_op jit(solution)/shard_map/pallas_call | solution.py:1245
  216.1 6.4 %shard_map.445 = (bf16[4,256,768]{2,1,0:T(8,128)(2,1)S(1)}, f32[8,384]{1,0:T(8,128)S(1)}, f32[8,256]{1,0:T(8,128)S(1)}, f32[8,128]{1,0:T(8,128)S(1)}) custom-call(s32[1]{0:T(128)} %bitcast.refs_0_, bf16[1024,640]{1,0:T(8,128)(2,1)S(1)} %get-tuple-element.172.refs_1_, f32[1024,384]{1,0:T(8,128)S(1)} %get-tuple-element.173.refs_1_.refs_2_, ...), custom_call_target="tpu_custom_call" | custom-call | flops 7000000000 | tf_op jit(solution)/shard_map/pallas_call | solution.py:1245
  226.1 4.9 %collective-permute-done.51.refs_6_.refs_2_ = bf16[144,768]{1,0:T(8,128)(2,1)S(1)} collective-permute-done((bf16[144,768]{1,0:T(8,128)(2,1)S(1)}, bf16[144,768]{1,0:T(8,128)(2,1)S(1)}, u32[]{:S(2)}, u32[]{:S(2)}) %collective-permute-start.51) | collective-permute-done | bytes 221216 | tf_op jit(solution)/shard_map/ppermute | solution.py:45
  231.0 4.5 %shard_map.448 = (f32[512,1024]{1,0:T(8,128)S(1)}, bf16[512,1024]{1,0:T(8,128)(2,1)S(1)}, f32[8,128]{1,0:T(8,128)S(1)}) custom-call(s32[1]{0:T(128)} %constant.88.clone.1.refs_0_, bf16[4,256,384]{2,1,0:T(8,128)(2,1)S(1)} %get-tuple-element.167.refs_1_, bf16[4,256,256]{2,1,0:T(8,128)(2,1)S(1)} %shard_map.440.refs_5_.refs_2_, ...), custom_call_target="tpu_custom_call" | custom-call | flops 4000000000 | tf_op jit(solution)/shard_map/pallas_call | solution.py:1245
  241.6 2.7 shard_map.455
  268.2 2.8 shard_map.453.refs_7_
  271.0 2.7 shard_map.458
  (404 shorter events, 147.8 us)
Async XLA Ops:
  16.5 24.0 %collective-permute-start.3 = (bf16[256,1024]{1,0:T(8,128)(2,1)S(1)}, bf16[256,1024]{1,0:T(8,128)(2,1)S(1)}, u32[]{:S(2)}, u32[]{:S(2)}) collective-permute-start(bf16[256,1024]{1,0:T(8,128)(2,1)S(1)} %get-tuple-element.129.refs_1_), channel_id=1, source_target_pairs={{0,2},{1,3},{2,0},{3,1},{4,6},{5,7},{6,4},{7,5},{8,10},{9,11},{10,... | collective-permute-start | bytes 1572872 | tf_op jit(solution)/shard_map/ppermute | solution.py:45
  16.8 16.2 %collective-permute-start.4 = (bf16[256,1024]{1,0:T(8,128)(2,1)S(1)}, bf16[256,1024]{1,0:T(8,128)(2,1)}, u32[]{:S(2)}, u32[]{:S(2)}) collective-permute-start(bf16[256,1024]{1,0:T(8,128)(2,1)S(1)} %get-tuple-element.129.refs_1_), channel_id=1, source_target_pairs={{0,1},{1,0},{2,3},{3,2},{4,5},{5,4},{6,7},{7,6},{8,9},{9,8},{10,11... | collective-permute-start | bytes 1572872 | tf_op jit(solution)/shard_map/ppermute | solution.py:45
  40.5 17.6 %collective-permute-start.5 = (bf16[256,1024]{1,0:T(8,128)(2,1)S(1)}, bf16[256,1024]{1,0:T(8,128)(2,1)}, u32[]{:S(2)}, u32[]{:S(2)}) collective-permute-start(bf16[256,1024]{1,0:T(8,128)(2,1)S(1)} %collective-permute-done.3.refs_2_), channel_id=1, source_target_pairs={{0,1},{1,0},{2,3},{3,2},{4,5},{5,4},{6,7},{7,6},{8,9},{9,8},{10,11... | collective-permute-start | bytes 1572872 | tf_op jit(solution)/shard_map/ppermute | solution.py:45
  62.9 33.3 %collective-permute-start.22 = (bf16[256,1024]{1,0:T(8,128)(2,1)S(1)}, bf16[256,1024]{1,0:T(8,128)(2,1)S(1)}, u32[]{:S(2)}, u32[]{:S(2)}) collective-permute-start(bf16[256,1024]{1,0:T(8,128)(2,1)S(1)} %shard_map.423.refs_3_), channel_id=1, source_target_pairs={{0,2},{1,3},{2,0},{3,1},{4,6},{5,7},{6,4},{7,5},{8,10},{9,11},{10,... | collective-permute-start | bytes 1572872 | tf_op jit(solution)/shard_map/ppermute | solution.py:45
  65.9 16.6 %collective-permute-start.20 = (bf16[128,1536]{1,0:T(8,128)(2,1)S(1)}, bf16[128,1536]{1,0:T(8,128)(2,1)S(1)}, u32[]{:S(2)}, u32[]{:S(2)}) collective-permute-start(bf16[128,1536]{1,0:T(8,128)(2,1)S(1)} %shard_map.421), channel_id=1, source_target_pairs={{0,8},{4,12},{8,16},{12,20},{16,24},{20,28},{24,0},{28,4},{1,9},{5... | collective-permute-start | bytes 1179656 | tf_op jit(solution)/shard_map/ppermute | solution.py:49
  66.9 15.7 %collective-permute-start.21 = (bf16[128,1536]{1,0:T(8,128)(2,1)S(1)}, bf16[128,1536]{1,0:T(8,128)(2,1)S(1)}, u32[]{:S(2)}, u32[]{:S(2)}) collective-permute-start(bf16[128,1536]{1,0:T(8,128)(2,1)S(1)} %shard_map.421), channel_id=1, source_target_pairs={{0,4},{4,0},{8,12},{12,8},{16,20},{20,16},{24,28},{28,24},{1,5},{5... | collective-permute-start | bytes 1179656 | tf_op jit(solution)/shard_map/ppermute | solution.py:45
  82.6 22.0 %collective-permute-start.23 = (bf16[128,1536]{1,0:T(8,128)(2,1)S(1)}, bf16[128,1536]{1,0:T(8,128)(2,1)S(1)}, u32[]{:S(2)}, u32[]{:S(2)}) collective-permute-start(bf16[128,1536]{1,0:T(8,128)(2,1)S(1)} %shard_map.422.refs_18_), channel_id=1, source_target_pairs={{0,8},{4,12},{8,16},{12,20},{16,24},{20,28},{24,0},{28,4},{1,9},{5... | collective-permute-start | bytes 1179656 | tf_op jit(solution)/shard_map/ppermute | solution.py:49
  108.9 14.9 %collective-permute-start.26 = (bf16[256,1024]{1,0:T(8,128)(2,1)S(1)}, bf16[256,1024]{1,0:T(8,128)(2,1)S(1)}, u32[]{:S(2)}, u32[]{:S(2)}) collective-permute-start(bf16[256,1024]{1,0:T(8,128)(2,1)S(1)} %shard_map.427), channel_id=1, source_target_pairs={{0,2},{1,3},{2,0},{3,1},{4,6},{5,7},{6,4},{7,5},{8,10},{9,11},{10,... | collective-permute-start | bytes 1572872 | tf_op jit(solution)/shard_map/ppermute | solution.py:45
  110.4 12.9 %collective-permute-start.27 = (bf16[128,1536]{1,0:T(8,128)(2,1)S(1)}, bf16[128,1536]{1,0:T(8,128)(2,1)S(1)}, u32[]{:S(2)}, u32[]{:S(2)}) collective-permute-start(bf16[128,1536]{1,0:T(8,128)(2,1)S(1)} %shard_map.426.refs_2_), channel_id=1, source_target_pairs={{0,8},{4,12},{8,16},{12,20},{16,24},{20,28},{24,0},{28,4},{1,9},{5... | collective-permute-start | bytes 1179656 | tf_op jit(solution)/shard_map/ppermute | solution.py:49
  113.5 13.1 %collective-permute-start.31 = (bf16[256,1024]{1,0:T(8,128)(2,1)S(1)}, bf16[256,1024]{1,0:T(8,128)(2,1)S(1)}, u32[]{:S(2)}, u32[]{:S(2)}) collective-permute-start(bf16[256,1024]{1,0:T(8,128)(2,1)S(1)} %shard_map.423.refs_3_), channel_id=1, source_target_pairs={{0,1},{1,0},{2,3},{3,2},{4,5},{5,4},{6,7},{7,6},{8,9},{9,8},{10,11... | collective-permute-start | bytes 1572872 | tf_op jit(solution)/shard_map/ppermute | solution.py:45
  125.4 14.3 %collective-permute-start.29 = (bf16[256,1024]{1,0:T(8,128)(2,1)S(1)}, bf16[256,1024]{1,0:T(8,128)(2,1)S(1)}, u32[]{:S(2)}, u32[]{:S(2)}) collective-permute-start(bf16[256,1024]{1,0:T(8,128)(2,1)S(1)} %get-tuple-element.144.refs_1_), channel_id=1, source_target_pairs={{0,2},{1,3},{2,0},{3,1},{4,6},{5,7},{6,4},{7,5},{8,10},{9,11},{10,... | collective-permute-start | bytes 1572872 | tf_op jit(solution)/shard_map/ppermute | solution.py:45
  126.6 13.7 %collective-permute-start.34 = (bf16[256,1024]{1,0:T(8,128)(2,1)S(1)}, bf16[256,1024]{1,0:T(8,128)(2,1)S(1)}, u32[]{:S(2)}, u32[]{:S(2)}) collective-permute-start(bf16[256,1024]{1,0:T(8,128)(2,1)S(1)} %collective-permute-done.22.refs_19_.refs_3_), channel_id=1, source_target_pairs={{0,1},{1,0},{2,3},{3,2},{4,5},{5,4},{6,7},{7,6},{8,9},{9,8},{10,11... | collective-permute-start | bytes 1572872 | tf_op jit(solution)/shard_map/ppermute | solution.py:45
  147.9 14.3 %collective-permute-start.37 = (bf16[256,1024]{1,0:T(8,128)(2,1)S(1)}, bf16[256,1024]{1,0:T(8,128)(2,1)S(1)}, u32[]{:S(2)}, u32[]{:S(2)}) collective-permute-start(bf16[256,1024]{1,0:T(8,128)(2,1)S(1)} %add_convert_fusion.2), channel_id=1, source_target_pairs={{0,2},{1,3},{2,0},{3,1},{4,6},{5,7},{6,4},{7,5},{8,10},{9,11},{10,... | collective-permute-start | bytes 1572872 | tf_op jit(solution)/shard_map/ppermute | solution.py:45
  163.3 14.6 %collective-permute-start.39 = (bf16[256,1024]{1,0:T(8,128)(2,1)S(1)}, bf16[256,1024]{1,0:T(8,128)(2,1)S(1)}, u32[]{:S(2)}, u32[]{:S(2)}) collective-permute-start(bf16[256,1024]{1,0:T(8,128)(2,1)S(1)} %get-tuple-element.159.refs_2_), channel_id=1, source_target_pairs={{0,2},{1,3},{2,0},{3,1},{4,6},{5,7},{6,4},{7,5},{8,10},{9,11},{10,... | collective-permute-start | bytes 1572872 | tf_op jit(solution)/shard_map/ppermute | solution.py:45
  178.6 18.4 %collective-permute-start.46 = (bf16[128,1536]{1,0:T(8,128)(2,1)S(1)}, bf16[128,1536]{1,0:T(8,128)(2,1)S(1)}, u32[]{:S(2)}, u32[]{:S(2)}) collective-permute-start(bf16[128,1536]{1,0:T(8,128)(2,1)S(1)} %get-tuple-element.178), channel_id=1, source_target_pairs={{0,4},{4,0},{8,12},{12,8},{16,20},{20,16},{24,28},{28,24},{1,5},{5... | collective-permute-start | bytes 1179656 | tf_op jit(solution)/shard_map/ppermute | solution.py:45
  179.5 17.5 %collective-permute-start.47 = (bf16[128,1536]{1,0:T(8,128)(2,1)S(1)}, bf16[128,1536]{1,0:T(8,128)(2,1)S(1)}, u32[]{:S(2)}, u32[]{:S(2)}) collective-permute-start(bf16[128,1536]{1,0:T(8,128)(2,1)S(1)} %get-tuple-element.163.refs_9_), channel_id=1, source_target_pairs={{0,8},{4,12},{8,16},{12,20},{16,24},{20,28},{24,0},{28,4},{1,9},{5... | collective-permute-start | bytes 1179656 | tf_op jit(solution)/shard_map/ppermute | solution.py:49
  185.0 14.5 %collective-permute-start.44 = (bf16[512,1024]{1,0:T(8,128)(2,1)S(1)}, bf16[512,1024]{1,0:T(8,128)(2,1)S(1)}, u32[]{:S(2)}, u32[]{:S(2)}) collective-permute-start(bf16[512,1024]{1,0:T(8,128)(2,1)S(1)} %get-tuple-element.166), channel_id=1, source_target_pairs={{0,1},{1,0},{2,3},{3,2},{4,5},{5,4},{6,7},{7,6},{8,9},{9,8},{10,11... | collective-permute-start | bytes 3145736 | tf_op jit(solution)/shard_map/ppermute | solution.py:45
  196.2 16.7 %collective-permute-start.48 = (bf16[128,1152]{1,0:T(8,128)(2,1)S(1)}, bf16[128,1152]{1,0:T(8,128)(2,1)S(1)}, u32[]{:S(2)}, u32[]{:S(2)}) collective-permute-start(bf16[128,1152]{1,0:T(8,128)(2,1)S(1)} %shard_map.442.refs_11_), channel_id=1, source_target_pairs={{0,4},{4,0},{8,12},{12,8},{16,20},{20,16},{24,28},{28,24},{1,5},{5... | collective-permute-start | bytes 884744 | tf_op jit(solution)/shard_map/ppermute | solution.py:45
  197.6 18.4 %collective-permute-start.49 = (bf16[128,1536]{1,0:T(8,128)(2,1)S(1)}, bf16[128,1536]{1,0:T(8,128)(2,1)S(1)}, u32[]{:S(2)}, u32[]{:S(2)}) collective-permute-start(bf16[128,1536]{1,0:T(8,128)(2,1)S(1)} %get-tuple-element.188), channel_id=1, source_target_pairs={{0,4},{4,0},{8,12},{12,8},{16,20},{20,16},{24,28},{28,24},{1,5},{5... | collective-permute-start | bytes 1179656 | tf_op jit(solution)/shard_map/ppermute | solution.py:45
  198.9 17.1 %collective-permute-start.50 = (bf16[128,1536]{1,0:T(8,128)(2,1)S(1)}, bf16[128,1536]{1,0:T(8,128)(2,1)S(1)}, u32[]{:S(2)}, u32[]{:S(2)}) collective-permute-start(bf16[128,1536]{1,0:T(8,128)(2,1)S(1)} %get-tuple-element.179.refs_10_), channel_id=1, source_target_pairs={{0,8},{4,12},{8,16},{12,20},{16,24},{20,28},{24,0},{28,4},{1,9},{5... | collective-permute-start | bytes 1179656 | tf_op jit(solution)/shard_map/ppermute | solution.py:49
  199.8 16.3 %collective-permute-start.45 = (bf16[256,1024]{1,0:T(8,128)(2,1)S(1)}, bf16[256,1024]{1,0:T(8,128)(2,1)S(1)}, u32[]{:S(2)}, u32[]{:S(2)}) collective-permute-start(bf16[256,1024]{1,0:T(8,128)(2,1)S(1)} %add_convert_fusion.1.refs_12_), channel_id=1, source_target_pairs={{0,2},{1,3},{2,0},{3,1},{4,6},{5,7},{6,4},{7,5},{8,10},{9,11},{10,... | collective-permute-start | bytes 1572872 | tf_op jit(solution)/shard_map/ppermute | solution.py:45
  240.7 22.8 %collective-permute-start.55 = (bf16[256,1024]{1,0:T(8,128)(2,1)}, bf16[256,1024]{1,0:T(8,128)(2,1)}, u32[]{:S(2)}, u32[]{:S(2)}) collective-permute-start(bf16[256,1024]{1,0:T(8,128)(2,1)} %add_convert_fusion.refs_5_.refs_6_), channel_id=1, source_target_pairs={{0,2},{1,3},{2,0},{3,1},{4,6},{5,7},{6,4},{7,5},{8,10},{9,11},{10,... | collective-permute-start | bytes 1572872 | tf_op jit(solution)/shard_map/ppermute | solution.py:45
  244.3 14.4 %collective-permute-start.62 = (bf16[128,1152]{1,0:T(8,128)(2,1)}, bf16[128,1152]{1,0:T(8,128)(2,1)}, u32[]{:S(2)}, u32[]{:S(2)}) collective-permute-start(bf16[128,1152]{1,0:T(8,128)(2,1)} %get-tuple-element.210), channel_id=1, source_target_pairs={{0,4},{4,0},{8,12},{12,8},{16,20},{20,16},{24,28},{28,24},{1,5},{5... | collective-permute-start | bytes 884744 | tf_op jit(solution)/shard_map/ppermute | solution.py:45
  245.6 13.2 %collective-permute-start.63 = (bf16[128,1152]{1,0:T(8,128)(2,1)}, bf16[128,1152]{1,0:T(8,128)(2,1)}, u32[]{:S(2)}, u32[]{:S(2)}) collective-permute-start(bf16[128,1152]{1,0:T(8,128)(2,1)} %get-tuple-element.211), channel_id=1, source_target_pairs={{0,8},{4,12},{8,16},{12,20},{16,24},{20,28},{24,0},{28,4},{1,9},{5... | collective-permute-start | bytes 884744 | tf_op jit(solution)/shard_map/ppermute | solution.py:49
  (127 other events, 1517.9 us)
